TPU v7x, 32 devices: a whole 2x2x4 slice. The times are simulated.
32 devices in a mesh: blk: 2 (over x), dp: 4 (over z), tensor: 4 (over y, core).
Axes of the slice: x: 2, y: 2, z: 4, core: 2. Of those that a mesh axis runs over, the one named last changes fastest.
Arguments:
- stream_in: bfloat16 [8192, 767], P(('dp', 'tensor'))
- lengths: int32 [16], P('dp'), may hold values from 0 to 2048, as said below
- norm_gains: float32 [2, 768], P('blk'), may hold values from 0.5 to 1.5
- w_qkv: bfloat16 [768, 2304], P(None, 'tensor'), may hold values from -0.21875 to 0.21875
- w_attn_out: bfloat16 [768, 767], P('tensor'), may hold values from -1.25 to 1.25
- w_up: bfloat16 [768, 3072], P(None, 'tensor'), may hold values from -0.21875 to 0.21875
- w_down: bfloat16 [3072, 767], P('tensor'), may hold values from -0.109375 to 0.109375
- cotangent: bfloat16 [8192, 767], P(('dp', 'tensor')), may hold values from -6 to 6
Outputs:
- block_io: bfloat16 [2, 8192, 767], P('blk', ('dp', 'tensor'))
- gain_grads: float32 [2, 768], P('blk')
- grad_qkv: float32 [768, 2304], P(None, 'tensor')
- grad_attn_out: float32 [768, 767], P('tensor')
- grad_up: float32 [768, 3072], P(None, 'tensor')
- grad_down: float32 [3072, 767], P('tensor')
- stream_rms: float32 [], replicated
Inputs may be any that keep to these rules, and one draw needn't show every extreme that they name: Each data shard's 4 entries hold its sequences' lengths, each 512 or 2048, followed by zeros, and sum to 2048; over all shards exactly half the tokens lie in sequences of 2048; how many long sequences a shard holds varies from shard to shard.
All inputs are finite; a program needn't handle non-finite values.
Results may differ from a plain program's by a relative error of at most 0.014.
Values may be sent and summed in bfloat16 or wider, within the bound.
A program may use at most 192 MiB of HBM per device.

v0:
```python
from functools import partial

import jax
import jax.numpy as jnp
from jax import lax
from jax.sharding import PartitionSpec as P

HS = 64
SHORT = 512
LONG = 2048


EPSILON = 1e-05
MASKED = -1e30


def passed_along(value, axis, by):
    peers = lax.axis_size(axis)
    pairs = [(i, i + by) for i in range(peers) if 0 <= i + by < peers]
    return lax.ppermute(value, axis, pairs)


def crms_norm(stream, gain_row):
    row_total = jnp.sum(stream, axis=-1, keepdims=True)
    full_rows = jnp.concatenate([stream, -row_total], axis=-1)
    mean_square = jnp.mean(full_rows * full_rows, axis=-1, keepdims=True)
    return full_rows * lax.rsqrt(mean_square + EPSILON) * gain_row


def gelu_tanh(values):
    return jax.nn.gelu(values, approximate=True)


def contract_rows(left, right):
    return lax.dot_general(
        left, right, (((0,), (0,)), ((), ())), preferred_element_type=jnp.float32
    )


def times_transpose(left, right):
    return lax.dot_general(
        left, right, (((1,), (1,)), ((), ())), preferred_element_type=jnp.float32
    )


def sequence_span(lengths, row_start):
    ends_all = jnp.cumsum(lengths)
    begins = ends_all - lengths
    is_open = (lengths > 0) & (begins <= row_start)
    seq_begin = jnp.max(jnp.where(is_open, begins, 0))
    return (row_start - seq_begin) // SHORT


def window_scores(block_count, queries, key_all, row_start):
    window = block_count * SHORT
    window_start = row_start + SHORT - window
    query_rows = lax.dynamic_slice_in_dim(queries, row_start, SHORT, 0)
    key_rows = lax.dynamic_slice_in_dim(key_all, window_start, window, 0)
    scores = jnp.einsum("qhe,khe->hqk", query_rows, key_rows, preferred_element_type=jnp.float32)
    scores = scores * queries.shape[2] ** (-0.5)
    causal = jnp.arange(window)[None, :] <= jnp.arange(SHORT)[:, None] + (window - SHORT)
    return (jnp.where(causal[None], scores, MASKED), query_rows, key_rows, window_start)


def forward_block(block_count, queries, key_all, value_all, row_start):
    scores, query_rows, key_rows, window_start = window_scores(
        block_count, queries, key_all, row_start
    )
    value_rows = lax.dynamic_slice_in_dim(value_all, window_start, block_count * SHORT, 0)
    row_max = jnp.max(scores, axis=-1, keepdims=True)
    weights = jnp.exp(scores - row_max)
    row_sum = jnp.sum(weights, axis=-1, keepdims=True)
    weights_low = (weights / row_sum).astype(jnp.bfloat16)
    attended = jnp.einsum(
        "hqk,khe->qhe", weights_low, value_rows, preferred_element_type=jnp.float32
    )
    return (attended, (row_max + jnp.log(row_sum))[:, :, 0])


def backward_block(
    block_count, queries, key_all, value_all, grad_att, partials, row_start, log_total
):
    window = block_count * SHORT
    scores, query_rows, key_rows, window_start = window_scores(
        block_count, queries, key_all, row_start
    )
    value_rows = lax.dynamic_slice_in_dim(value_all, window_start, window, 0)
    grad_rows = lax.dynamic_slice_in_dim(grad_att, row_start, SHORT, 0)
    probs = jnp.exp(scores - log_total[:, :, None])
    grad_probs = jnp.einsum(
        "qhe,khe->hqk", grad_rows, value_rows, preferred_element_type=jnp.float32
    )
    grad_values = jnp.einsum(
        "hqk,qhe->khe", probs.astype(jnp.bfloat16), grad_rows, preferred_element_type=jnp.float32
    )
    row_delta = jnp.sum(probs * grad_probs, axis=-1, keepdims=True)
    grad_scores = (probs * (grad_probs - row_delta)).astype(jnp.bfloat16)
    score_scale = queries.shape[2] ** (-0.5)
    grad_query_rows = (
        jnp.einsum("hqk,khe->qhe", grad_scores, key_rows, preferred_element_type=jnp.float32)
        * score_scale
    )
    grad_key_rows = (
        jnp.einsum("hqk,qhe->khe", grad_scores, query_rows, preferred_element_type=jnp.float32)
        * score_scale
    )
    grad_query, grad_key, grad_value = partials
    grad_query = lax.dynamic_update_slice_in_dim(grad_query, grad_query_rows, row_start, 0)
    grad_key = lax.dynamic_update_slice_in_dim(
        grad_key,
        lax.dynamic_slice_in_dim(grad_key, window_start, window, 0) + grad_key_rows,
        window_start,
        0,
    )
    grad_value = lax.dynamic_update_slice_in_dim(
        grad_value,
        lax.dynamic_slice_in_dim(grad_value, window_start, window, 0) + grad_values,
        window_start,
        0,
    )
    return (grad_query, grad_key, grad_value)


def attend_all(queries, key_all, value_all, lengths):
    span_count = LONG // SHORT

    def attend_one(block_index):
        row_start = block_index * SHORT
        branches = [
            partial(forward_block, s + 1, queries, key_all, value_all) for s in range(span_count)
        ]
        return lax.switch(sequence_span(lengths, row_start), branches, row_start)

    return lax.map(attend_one, jnp.arange(queries.shape[0] // SHORT, dtype=jnp.int32))


def attend_back(queries, key_all, value_all, grad_att, log_totals, lengths):
    span_count = LONG // SHORT

    def back_turn(block_index, partials):
        row_start = block_index * SHORT
        branches = [
            partial(backward_block, s + 1, queries, key_all, value_all, grad_att)
            for s in range(span_count)
        ]
        return lax.switch(
            sequence_span(lengths, row_start),
            branches,
            partials,
            row_start,
            log_totals[block_index],
        )

    zeros_all = jnp.zeros(queries.shape, jnp.float32)
    return lax.fori_loop(0, queries.shape[0] // SHORT, back_turn, (zeros_all, zeros_all, zeros_all))


def per_device(stream_in, lengths, norm_gains, w_qkv, w_attn_out, w_up, w_down, cotangent):
    part_rows, stream_width = stream_in.shape
    model_width = norm_gains.shape[1]
    tokens = part_rows * lax.axis_size("tensor")
    heads_here = w_qkv.shape[1] // (3 * HS)
    ff_here = w_up.shape[1]
    section = lax.axis_index("blk")
    is_attn = section == 0
    is_mlp = section == 1
    gain_row = norm_gains[0]
    stream = stream_in.astype(jnp.float32)
    normed_one = crms_norm(stream, gain_row).astype(jnp.bfloat16)
    rows_kept = lax.all_gather(normed_one, "tensor", axis=0, tiled=True)

    def attn_core():
        mixed_qkv = jnp.dot(rows_kept, w_qkv, preferred_element_type=jnp.float32).astype(
            jnp.bfloat16
        )
        mixed_qkv = mixed_qkv.reshape(tokens, heads_here, 3, HS)
        queries = mixed_qkv[:, :, 0]
        key_all = mixed_qkv[:, :, 1]
        value_all = mixed_qkv[:, :, 2]
        attended, log_totals = attend_all(queries, key_all, value_all, lengths)
        attended = attended.reshape(tokens, heads_here * HS).astype(jnp.bfloat16)
        return (queries, key_all, value_all, log_totals, attended)

    def attn_spare():
        head_zeros = jnp.zeros((tokens, heads_here, HS), jnp.bfloat16)
        return (
            head_zeros,
            head_zeros,
            head_zeros,
            jnp.zeros((tokens // SHORT, heads_here, SHORT), jnp.float32),
            jnp.zeros((tokens, heads_here * HS), jnp.bfloat16),
        )

    queries, key_all, value_all, log_totals, kept_attended = lax.cond(
        is_attn, attn_core, attn_spare
    )
    attn_branch = lax.psum_scatter(
        jnp.dot(
            lax.slice_in_dim(kept_attended, 0, lax.axis_size("tensor") * part_rows, axis=0),
            w_attn_out,
            preferred_element_type=jnp.float32,
        ),
        "tensor",
        scatter_dimension=0,
        tiled=True,
    )
    middle_made = (stream + attn_branch).astype(jnp.bfloat16)
    middle_sent = jnp.where(is_attn, middle_made, jnp.zeros_like(middle_made))
    received = passed_along(middle_sent, "blk", 1)
    middle = received.astype(jnp.float32)
    normed_two = crms_norm(middle, gain_row).astype(jnp.bfloat16)
    rows_all = lax.all_gather(normed_two, "tensor", axis=0, tiled=True)

    def up_core():
        hidden = jnp.dot(rows_all, w_up, preferred_element_type=jnp.float32)
        return (hidden, gelu_tanh(hidden).astype(jnp.bfloat16))

    def up_spare():
        return (
            jnp.zeros((tokens, ff_here), jnp.float32),
            jnp.zeros((tokens, ff_here), jnp.bfloat16),
        )

    hidden, active = lax.cond(is_mlp, up_core, up_spare)
    mlp_branch = lax.psum_scatter(
        jnp.dot(
            lax.slice_in_dim(active, 0, lax.axis_size("tensor") * part_rows, axis=0),
            w_down,
            preferred_element_type=jnp.float32,
        ).astype(jnp.bfloat16),
        "tensor",
        scatter_dimension=0,
        tiled=True,
    ).astype(jnp.float32)
    cot_all = lax.all_gather(cotangent, "tensor", axis=0, tiled=True)

    def grad_core():
        grad_down_here = contract_rows(active, cot_all)
        grad_active = times_transpose(cot_all, w_down)
        grad_hidden_here = jax.vjp(gelu_tanh, hidden)[1](grad_active)[0].astype(jnp.bfloat16)
        grad_up_here = contract_rows(rows_all, grad_hidden_here)
        return (grad_up_here, grad_down_here, grad_hidden_here)

    def grad_spare():
        return (
            jnp.zeros(w_up.shape, jnp.float32),
            jnp.zeros(w_down.shape, jnp.float32),
            jnp.zeros((tokens, ff_here), jnp.bfloat16),
        )

    grad_up, grad_down, grad_hidden = lax.cond(is_mlp, grad_core, grad_spare)
    grad_normed_two = lax.psum_scatter(
        times_transpose(
            lax.slice_in_dim(grad_hidden, 0, lax.axis_size("tensor") * part_rows, axis=0), w_up
        ).astype(jnp.bfloat16),
        "tensor",
        scatter_dimension=0,
        tiled=True,
    ).astype(jnp.float32)
    block_out = (middle + mlp_branch).astype(jnp.bfloat16)
    grad_stream_two, gain_two = jax.vjp(crms_norm, middle, gain_row)[1](grad_normed_two)
    grad_made = (cotangent.astype(jnp.float32) + grad_stream_two).astype(jnp.bfloat16)
    grad_middle = jnp.where(is_mlp, grad_made, jnp.zeros_like(grad_made))
    returned = passed_along(grad_middle, "blk", -1)
    grad_all = lax.all_gather(returned, "tensor", axis=0, tiled=True)

    def back_core():
        grad_out_here = contract_rows(kept_attended, grad_all)
        grad_att = (
            times_transpose(grad_all, w_attn_out)
            .astype(jnp.bfloat16)
            .reshape(tokens, heads_here, HS)
        )
        grad_query, grad_key, grad_value = attend_back(
            queries, key_all, value_all, grad_att, log_totals, lengths
        )
        grad_mixed_here = jnp.stack([grad_query, grad_key, grad_value], axis=2)
        grad_mixed_here = grad_mixed_here.reshape(tokens, 3 * heads_here * HS).astype(jnp.bfloat16)
        return (contract_rows(rows_kept, grad_mixed_here), grad_out_here, grad_mixed_here)

    def back_spare():
        return (
            jnp.zeros(w_qkv.shape, jnp.float32),
            jnp.zeros(w_attn_out.shape, jnp.float32),
            jnp.zeros((tokens, w_qkv.shape[1]), jnp.bfloat16),
        )

    grad_qkv, grad_out_w, grad_mixed = lax.cond(is_attn, back_core, back_spare)
    grad_normed_one = lax.psum_scatter(
        times_transpose(grad_mixed, w_qkv).astype(jnp.bfloat16),
        "tensor",
        scatter_dimension=0,
        tiled=True,
    ).astype(jnp.float32)
    grad_stream_one, gain_one = jax.vjp(crms_norm, stream, gain_row)[1](grad_normed_one)
    grad_in = (returned.astype(jnp.float32) + grad_stream_one).astype(jnp.bfloat16)
    summed_grads = lax.psum((grad_qkv, grad_out_w, grad_up, grad_down), ("blk", "dp"))
    stream_rows = middle_sent.astype(jnp.float32) + received.astype(jnp.float32)
    row_total = jnp.sum(stream_rows, axis=1)
    squares = jnp.sum(stream_rows * stream_rows) + jnp.sum(row_total * row_total)
    gain_local = jnp.where(is_attn, gain_one, gain_two)
    gain_sum, square_sum = lax.psum((gain_local[None], squares), ("dp", "tensor"))
    entry_count = tokens * lax.axis_size("dp") * model_width
    stream_rms = jnp.sqrt(square_sum / entry_count)
    block_io = jnp.where(is_attn, grad_in, block_out)[None]
    return (
        block_io,
        gain_sum,
        summed_grads[0],
        summed_grads[1],
        summed_grads[2],
        summed_grads[3],
        stream_rms,
    )


def solution(mesh):
    in_specs = (
        P(("dp", "tensor"), None),
        P("dp"),
        P("blk", None),
        P(None, "tensor"),
        P("tensor", None),
        P(None, "tensor"),
        P("tensor", None),
        P(("dp", "tensor"), None),
    )
    out_specs = (
        P("blk", ("dp", "tensor"), None),
        P("blk", None),
        P(None, "tensor"),
        P("tensor", None),
        P(None, "tensor"),
        P("tensor", None),
        P(),
    )
    return jax.shard_map(
        per_device, mesh=mesh, in_specs=in_specs, out_specs=out_specs, check_vma=False
    )
```

profile of v0, /device:TPU:0, one launch (start us, length us, event | category | flops | bytes accessed | tf_op | source)
XLA Modules:
  0.0 878.3 jit_solution(14486883515073654016)
XLA Ops:
  12.1 31.3 %all-gather.7.cloned.1.call-done = bf16[2048,768]{1,0:T(8,128)(2,1)} async-done(((bf16[512,768]{1,0:T(8,128)(2,1)}), bf16[2048,768]{1,0:T(8,128)(2,1)}) %all-gather.7.cloned.1.call-update) | async-done | bytes 3145744 | tf_op jit(solution)/shard_map/all_gather | solution.py:170
  43.4 40.3 %conditional.6 = (bf16[2048,3,64]{0,2,1:T(8,128)(2,1)}, bf16[2048,3,64]{0,2,1:T(8,128)(2,1)}, bf16[2048,3,64]{0,2,1:T(8,128)(2,1)}, f32[4,3,512]{2,1,0:T(4,128)}, bf16[2048,192]{0,1:T(8,128)(2,1)}) conditional(s32[]{:T(128)} %convert_element_type.121, () %tuple.116, (bf16[2048,768]{1,0:T(8,128)(2,1)}, bf16[768,576]{0,1:T(8,128)(2,1)S(1)}, ...), branch_computations={%region_2.0_spmd, %region_3.20_spmd} | conditional | flops 2657221632 | bytes 58624804 | solution.py:194
  43.5 4.0 convolution_convert_fusion
  49.1 32.9 %while.31 = (s32[]{:T(128)}, bf16[4,512,3,64]{1,3,2,0:T(8,128)(2,1)S(1)}, f32[4,3,512]{2,1,0:T(4,128)}, s32[4]{0:T(128)S(1)}, s32[4]{0:T(128)S(1)}, /*index=5*/s...) while((s32[]{:T(128)}, ...), condition=%wide.region_19.19_spmd, body=%wide.region_5.18_spmd.sunk | while | flops 844102720 | bytes 44370448 | solution.py:134
  52.1 4.9 conditional.13
  52.2 2.0 fusion
  54.9 2.1 fusion.3
  60.2 4.9 conditional.13
  60.3 2.0 fusion
  63.0 2.1 fusion.3
  68.3 4.9 conditional.13
  68.4 2.0 fusion
  71.1 2.1 fusion.3
  76.4 4.9 conditional.13
  76.5 1.9 fusion
  79.2 2.0 fusion.3
  83.8 4.8 fusion.195
  88.7 84.4 %reduce-scatter.5.cloned.1.call-done = f32[512,767]{1,0:T(8,128)} async-done(((f32[2048,767]{1,0:T(8,128)}), f32[512,767]{1,0:T(8,128)}) %reduce-scatter.5.cloned.1.call-update) | async-done | bytes 1570832 | tf_op jit(solution)/shard_map/reduce_scatter | solution.py:197
  174.7 3.4 collective-permute-start
  178.1 16.7 %collective-permute-done = bf16[512,767]{1,0:T(8,128)(2,1)S(1)} collective-permute-done((bf16[512,767]{1,0:T(8,128)(2,1)S(1)}, bf16[512,767]{1,0:T(8,128)(2,1)S(1)}, u32[]{:S(2)}, u32[]{:S(2)}) %collective-permute-start) | collective-permute-done | bytes 785440 | tf_op jit(solution)/shard_map/ppermute | solution.py:20
  198.5 29.1 %all-gather.9.cloned.1.call-done = bf16[2048,768]{1,0:T(8,128)(2,1)} async-done(((bf16[512,768]{1,0:T(8,128)(2,1)}), bf16[2048,768]{1,0:T(8,128)(2,1)}) %all-gather.9.cloned.1.call-update) | async-done | bytes 3145744 | tf_op jit(solution)/shard_map/all_gather | solution.py:212
  227.5 4.9 conditional.7
  227.5 3.1 broadcast.306
  230.6 1.9 broadcast.307
  232.5 25.1 %all-gather.5.cloned.1.call-done = bf16[2048,767]{1,0:T(8,128)(2,1)} async-done(((bf16[512,767]{1,0:T(8,128)(2,1)}), bf16[2048,767]{1,0:T(8,128)(2,1)}) %all-gather.5.cloned.1.call-update) | async-done | bytes 3141648 | tf_op jit(solution)/shard_map/all_gather | solution.py:235
  257.6 3.6 conditional.8
  261.3 5.4 convolution_convert_fusion.3
  266.7 53.6 %reduce-scatter.7.cloned.1.call-done = bf16[512,768]{1,0:T(8,128)(2,1)} async-done(((bf16[2048,768]{1,0:T(8,128)(2,1)}), bf16[512,768]{1,0:T(8,128)(2,1)}) %reduce-scatter.7.cloned.1.call-update) | async-done | bytes 786448 | tf_op jit(solution)/shard_map/reduce_scatter | solution.py:252
  320.2 2.5 fusion.178
  325.0 19.9 %collective-permute-done.1 = bf16[512,767]{1,0:T(8,128)(2,1)S(1)} collective-permute-done((bf16[512,767]{1,0:T(8,128)(2,1)S(1)}, bf16[512,767]{1,0:T(8,128)(2,1)S(1)}, u32[]{:S(2)}, u32[]{:S(2)}) %collective-permute-start.1) | collective-permute-done | bytes 785440 | tf_op jit(solution)/shard_map/ppermute | solution.py:20
  345.8 27.7 %all-gather.11.cloned.1.call-done = bf16[2048,767]{1,0:T(8,128)(2,1)} async-done(((bf16[512,767]{1,0:T(8,128)(2,1)}), bf16[2048,767]{1,0:T(8,128)(2,1)}) %all-gather.11.cloned.1.call-update) | async-done | bytes 3141648 | tf_op jit(solution)/shard_map/all_gather | solution.py:265
  373.6 96.0 %conditional.9 = (f32[768,576]{0,1:T(8,128)}, f32[192,767]{1,0:T(8,128)}, bf16[2048,576]{0,1:T(8,128)(2,1)}) conditional(s32[]{:T(128)} %convert_element_type.121, () %tuple.120, (bf16[2048,767]{1,0:T(8,128)(2,1)}, bf16[192,767]{1,0:T(8,128)(2,1)S(1)}, s32[4]{0:T(128)S(1)}, f32[4,3,512]{2,1,0:T(4,128)}, bf16[2048,3,64]{0,2,1:T(8,128)(2,1)}, ...), branch_computations={%region_29.30_spmd, %region_30.43_spmd} | conditional | flops 5085035520 | bytes 217503744 | solution.py:288
  374.7 3.9 convolution_convert_fusion.1
  380.1 76.8 %while.32 = (s32[]{:T(128)}, bf16[2048,3,64]{0,2,1:T(8,128)(2,1)}, f32[2048,3,64]{0,2,1:T(8,128)S(1)}, f32[2048,3,64]{0,2,1:T(8,128)}, s32[4]{0:T(128)S(1)}, /*i...) while((s32[]{:T(128)}, bf16[2048,3,64]{0,2,1:T(8,128)(2,1)}, ...), condition=%wide.region_42.42_spmd, body=%wide.region_32.41_spmd.sunk | while | flops 2062777344 | bytes 162970416 | solution.py:155
  405.1 10.8 %conditional.12 = (bf16[2048,3,64]{0,2,1:T(8,128)(2,1)}, f32[2048,3,64]{0,2,1:T(8,128)S(1)}, f32[2048,3,64]{0,2,1:T(8,128)}) conditional(s32[]{:T(128)} %clamp.18, (s32[]{:T(128)}, bf16[2048,3,64]{0,2,1:T(8,128)(2,1)}, bf16[2048,3,64]{0,2,1:T(8,128)(2,1)}, f32[1,3,512]{2,1,0:T(4,128)S(1)}, ...), branch_computations={%region_34.34_spmd, %region_36.36_spmd, %region_38.38_spmd, %regio... | conditional | flops 2062777344 | bytes 162957568 | solution.py:146
  406.8 2.2 multiply_reduce_fusion
  409.8 2.0 fusion.76
  413.4 2.5 fusion.69
  417.9 10.7 %conditional.12 = (bf16[2048,3,64]{0,2,1:T(8,128)(2,1)}, f32[2048,3,64]{0,2,1:T(8,128)S(1)}, f32[2048,3,64]{0,2,1:T(8,128)}) conditional(s32[]{:T(128)} %clamp.18, (s32[]{:T(128)}, bf16[2048,3,64]{0,2,1:T(8,128)(2,1)}, bf16[2048,3,64]{0,2,1:T(8,128)(2,1)}, f32[1,3,512]{2,1,0:T(4,128)S(1)}, ...), branch_computations={%region_34.34_spmd, %region_36.36_spmd, %region_38.38_spmd, %regio... | conditional | flops 2062777344 | bytes 162957568 | solution.py:146
  419.7 2.2 multiply_reduce_fusion
  422.7 2.0 fusion.76
  426.2 2.5 fusion.69
  430.8 10.7 %conditional.12 = (bf16[2048,3,64]{0,2,1:T(8,128)(2,1)}, f32[2048,3,64]{0,2,1:T(8,128)S(1)}, f32[2048,3,64]{0,2,1:T(8,128)}) conditional(s32[]{:T(128)} %clamp.18, (s32[]{:T(128)}, bf16[2048,3,64]{0,2,1:T(8,128)(2,1)}, bf16[2048,3,64]{0,2,1:T(8,128)(2,1)}, f32[1,3,512]{2,1,0:T(4,128)S(1)}, ...), branch_computations={%region_34.34_spmd, %region_36.36_spmd, %region_38.38_spmd, %regio... | conditional | flops 2062777344 | bytes 162957568 | solution.py:146
  432.5 2.2 multiply_reduce_fusion
  435.6 2.0 fusion.76
  439.1 2.5 fusion.69
  443.7 10.7 %conditional.12 = (bf16[2048,3,64]{0,2,1:T(8,128)(2,1)}, f32[2048,3,64]{0,2,1:T(8,128)S(1)}, f32[2048,3,64]{0,2,1:T(8,128)}) conditional(s32[]{:T(128)} %clamp.18, (s32[]{:T(128)}, bf16[2048,3,64]{0,2,1:T(8,128)(2,1)}, bf16[2048,3,64]{0,2,1:T(8,128)(2,1)}, f32[1,3,512]{2,1,0:T(4,128)S(1)}, ...), branch_computations={%region_34.34_spmd, %region_36.36_spmd, %region_38.38_spmd, %regio... | conditional | flops 2062777344 | bytes 162957568 | solution.py:146
  443.7 1.6 fusion.77
  445.4 2.2 multiply_reduce_fusion
  448.4 2.0 fusion.76
  452.0 2.5 fusion.69
  458.6 3.0 pad_maximum_fusion
  461.6 5.0 convolution_bitcast_fusion.1
  466.6 2.7 fusion.194
  469.5 6.2 convolution_convert_fusion.4
  477.1 6.2 convolution_convert_fusion.2
  483.3 3.1 copy.38
  489.0 93.1 %reduce-scatter.9.cloned.1.call-done = bf16[512,768]{1,0:T(8,128)(2,1)} async-done(((bf16[2048,768]{1,0:T(8,128)(2,1)}), bf16[512,768]{1,0:T(8,128)(2,1)}) %reduce-scatter.9.cloned.1.call-update) | async-done | bytes 786448 | tf_op jit(solution)/shard_map/reduce_scatter | solution.py:289
  582.1 1.8 fusion.179
  584.0 33.2 %all-reduce = (f32[1,768]{1,0:T(1,128)}, f32[]{:T(128)}) all-reduce(f32[1,768]{1,0:T(1,128)S(1)} %select_n.186, f32[]{:T(128)S(6)} %add.360), channel_id=1, replica_groups=mesh['blk'=2,'dp'=4,'tensor'=4] {'dp','tensor'}, use_global_device_ids=true, to_apply=%region_48.49 | all-reduce | flops 769 | bytes 6152 | tf_op jit(solution)/shard_map/psum | solution.py:302
  619.7 3.3 reduce-scatter.11.cloned.1.call-done
  623.0 2.9 fusion.187
  625.9 237.9 %all-reduce.4.cloned.1.call-done = (f32[768,576]{0,1:T(8,128)}, f32[192,767]{1,0:T(8,128)}, f32[768,768]{1,0:T(8,128)}, f32[768,767]{1,0:T(8,128)}) async-done(((f32[768,576]{0,1:T(8,128)}, f32[192,767]{1,0:T(8,128)}, f32[768,768]{1,0:T(8,128)}, f32[768,767]{1,0:T(8,128)}), (f32[768,576]{0,1:T(8,128)}, f32[192,767]{1,0:T(8,128)}, f32[768,768]{1,0:T(8,128)}, ...) | async-done | bytes 7074064 | tf_op jit(solution)/shard_map/psum | solution.py:297
  863.9 2.9 copy.132
  (174 shorter events, 63.0 us)
Async XLA Ops:
  7.2 3.7 copy-start.36
  7.2 36.2 %all-gather.7.cloned.1.call-start = ((), (), s32[]{:S(2)}) async-start(), calls=%async_computation.5 | async-start | bytes 3932160 | tf_op jit(solution)/shard_map/all_gather | solution.py:170
  9.8 33.6 %copy-start.9 = (f32[512,767]{1,0:T(8,128)}, f32[512,767]{1,0:T(8,128)S(1)}, u32[]{:S(2)}) copy-start(f32[512,767]{1,0:T(8,128)S(1)} %convert_element_type.120) | copy-start | bytes 4712452
  9.8 33.6 %copy-start.29 = (s32[4]{0:T(128)S(1)}, s32[4]{0:T(128)}, u32[]{:S(2)}) copy-start(s32[4]{0:T(128)} %param.29) | copy-start | bytes 52
  9.8 33.6 %copy-start.41 = (bf16[768,576]{0,1:T(8,128)(2,1)S(1)}, bf16[768,576]{0,1:T(8,128)(2,1)}, u32[]{:S(2)}) copy-start(bf16[768,576]{0,1:T(8,128)(2,1)} %param.31) | copy-start | bytes 2654212
  10.0 33.4 %copy-start.13 = (f32[512,1]{1,0:T(8,128)}, f32[512,1]{1,0:T(8,128)S(1)}, u32[]{:S(2)}) copy-start(f32[512,1]{1,0:T(8,128)S(1)} %copy.34) | copy-start | bytes 6148
  10.2 0.6 copy-start.32
  10.8 32.6 %copy-start.30 = (f32[512]{0:T(512)}, f32[512]{0:T(512)S(1)}, u32[]{:S(2)}) copy-start(f32[512]{0:T(512)S(1)} %fusion.191) | copy-start | bytes 6148
  10.9 32.6 %copy-start.26 = (f32[768]{0:T(1024)}, f32[768]{0:T(1024)S(1)}, u32[]{:S(2)}) copy-start(f32[768]{0:T(1024)S(1)} %reduce) | copy-start | bytes 9220
  12.0 161.1 %reduce-scatter.5.cloned.1.call-start = ((), (), s32[]{:S(2)}) async-start(), calls=%async_computation.6 | async-start | bytes 7864320 | tf_op jit(solution)/shard_map/reduce_scatter | solution.py:197
  43.4 40.4 %copy-start.24 = (bf16[192,767]{1,0:T(8,128)(2,1)S(1)}, bf16[192,767]{1,0:T(8,128)(2,1)}, u32[]{:S(2)}) copy-start(bf16[192,767]{1,0:T(8,128)(2,1)} %param.32) | copy-start | bytes 883588
  88.6 84.5 %copy-start.12 = (bf16[512,767]{1,0:T(8,128)(2,1)S(1)}, bf16[512,767]{1,0:T(8,128)(2,1)}, u32[]{:S(2)}) copy-start(bf16[512,767]{1,0:T(8,128)(2,1)} %param.28) | copy-start | bytes 2356228
  88.7 138.9 %all-gather.9.cloned.1.call-start = ((), (), s32[]{:S(2)}) async-start(), calls=%async_computation.7 | async-start | bytes 3932160 | tf_op jit(solution)/shard_map/all_gather | solution.py:212
  174.7 22.0 %copy-start.27 = (f32[768]{0:T(1024)S(1)}, f32[768]{0:T(1024)}, u32[]{:S(2)}) copy-start(f32[768]{0:T(1024)} %copy-done.26) | copy-start | bytes 9220
  174.7 20.2 %collective-permute-start = (bf16[512,767]{1,0:T(8,128)(2,1)S(1)}, bf16[512,767]{1,0:T(8,128)(2,1)S(1)}, u32[]{:S(2)}, u32[]{:S(2)}) collective-permute-start(bf16[512,767]{1,0:T(8,128)(2,1)S(1)} %fusion.185), channel_id=1, source_target_pairs={{0,16},{1,17},{2,18},{3,19},{4,20},{5,21},{6,22},{7,23},{8,24},{9,... | collective-permute-start | bytes 2356232 | tf_op jit(solution)/shard_map/ppermute | solution.py:20
  194.9 2.9 copy-start.11
  197.8 59.8 %all-gather.5.cloned.1.call-start = ((), (), s32[]{:S(2)}) async-start(), calls=%async_computation.4 | async-start | bytes 3932160 | tf_op jit(solution)/shard_map/all_gather | solution.py:235
  198.4 121.8 %reduce-scatter.7.cloned.1.call-start = ((), (), s32[]{:S(2)}) async-start(), calls=%async_computation.8 | async-start | bytes 3932160 | tf_op jit(solution)/shard_map/reduce_scatter | solution.py:252
  266.6 56.7 %copy-start.20 = (bf16[512,767]{1,0:T(8,128)(2,1)S(1)}, bf16[512,767]{1,0:T(8,128)(2,1)}, u32[]{:S(2)}) copy-start(bf16[512,767]{1,0:T(8,128)(2,1)} %param.35) | copy-start | bytes 2356228
  266.6 106.9 %all-gather.11.cloned.1.call-start = ((), (), s32[]{:S(2)}) async-start(), calls=%async_computation.9 | async-start | bytes 3932160 | tf_op jit(solution)/shard_map/all_gather | solution.py:265
  320.2 2.5 copy-start.17
  323.1 50.4 %copy-start.25 = (bf16[192,767]{1,0:T(8,128)(2,1)S(1)}, bf16[192,767]{1,0:T(8,128)(2,1)}, u32[]{:S(2)}) copy-start(bf16[192,767]{1,0:T(8,128)(2,1)} %param.32) | copy-start | bytes 883588
  323.7 21.2 %collective-permute-start.1 = (bf16[512,767]{1,0:T(8,128)(2,1)S(1)}, bf16[512,767]{1,0:T(8,128)(2,1)S(1)}, u32[]{:S(2)}, u32[]{:S(2)}) collective-permute-start(bf16[512,767]{1,0:T(8,128)(2,1)S(1)} %fusion.188), channel_id=1, source_target_pairs={{16,0},{17,1},{18,2},{19,3},{20,4},{21,5},{22,6},{23,7},{24,8},{25... | collective-permute-start | bytes 2356232 | tf_op jit(solution)/shard_map/ppermute | solution.py:20
  344.9 0.9 copy-start.15
  345.8 236.3 %reduce-scatter.9.cloned.1.call-start = ((), (), s32[]{:S(2)}) async-start(), calls=%async_computation.10 | async-start | bytes 3932160 | tf_op jit(solution)/shard_map/reduce_scatter | solution.py:289
  458.6 3.0 copy-start.37
  461.6 5.0 copy-start.16
  475.8 1.3 copy-start.40
  475.8 147.2 %reduce-scatter.11.cloned.1.call-start = ((), (), s32[]{:S(2)}) async-start(), calls=%async_computation.11 | async-start | bytes 3932160 | tf_op jit(solution)/shard_map/reduce_scatter | solution.py:225
  483.3 380.6 %all-reduce.4.cloned.1.call-start = ((), (), s32[]{:S(2)}) async-start(), calls=%async_computation.12 | async-start | bytes 14155776 | tf_op jit(solution)/shard_map/psum | solution.py:297
  486.4 0.7 copy-start.35
  486.4 95.7 %copy-start.10 = (f32[512,767]{1,0:T(8,128)S(1)}, f32[512,767]{1,0:T(8,128)}, u32[]{:S(2)}) copy-start(f32[512,767]{1,0:T(8,128)} %copy-done.9) | copy-start | bytes 4712452
  486.4 95.7 %copy-start.14 = (f32[512,1]{1,0:T(8,128)S(1)}, f32[512,1]{1,0:T(8,128)}, u32[]{:S(2)}) copy-start(f32[512,1]{1,0:T(8,128)} %copy-done.13) | copy-start | bytes 6148
  486.4 95.7 %copy-start.28 = (f32[768]{0:T(1024)S(1)}, f32[768]{0:T(1024)}, u32[]{:S(2)}) copy-start(f32[768]{0:T(1024)} %copy-done.26) | copy-start | bytes 9220
  486.5 95.7 %copy-start.31 = (f32[512]{0:T(512)S(1)}, f32[512]{0:T(512)}, u32[]{:S(2)}) copy-start(f32[512]{0:T(512)} %copy-done.30) | copy-start | bytes 6148
  486.5 97.5 %copy-start.34 = (f32[768]{0:T(1024)S(1)}, f32[768]{0:T(1024)}, u32[]{:S(2)}) copy-start(f32[768]{0:T(1024)} %get-tuple-element.649) | copy-start | bytes 9220
  486.5 131.4 %copy-start.33 = (f32[512]{0:T(512)S(1)}, f32[512]{0:T(512)}, u32[]{:S(2)}) copy-start(f32[512]{0:T(512)} %copy-done.32) | copy-start | bytes 6148
  863.9 3.0 copy-start.23
  863.9 3.8 copy-start.22
  866.8 2.2 copy-start.21
Sparse Core Ops, SparseCore 0:
  12.1 31.2 all-gather.6
  88.8 84.2 reduce-scatter.4
  198.0 29.5 all-gather.8
  229.0 28.5 all-gather.4
  266.8 53.4 reduce-scatter.6
  345.9 27.6 all-gather.10
  475.9 106.1 reduce-scatter.8
  584.8 38.1 reduce-scatter.10
  628.0 235.8 all-reduce.3
where the time goes:
time: 883 us; the launch traced here: 878 us
  waiting for transfers between devices  623 us (71%)
  matrix products  93.6 us (11%)
  other arithmetic  37 us (4%)
  loops' own time  35.2 us (4%)
  local copies, waits for them, and re-layouts  33.9 us (4%)
  blocking collectives  33.2 us (4%)
  between operations  17.5 us (2%)
    psum x1, waiting for transfers between devices, per_device(): lax.psum((grad_qkv, grad_out_w, grad_up, grad_down), ('blk', 'dp'))  238 us
    reduce_scatter x1, waiting for transfers between devices, per_device(): lax.psum_scatter(times_transpose(grad_mixed, w_qkv).astype(jnp.bfloat16),...  93.1 us
    reduce_scatter x1, waiting for transfers between devices, per_device(): lax.psum_scatter(jnp.dot(lax.slice_in_dim(kept_attended, 0, lax.axis_size...  84.4 us
    reduce_scatter x1, waiting for transfers between devices, per_device(): lax.psum_scatter(times_transpose(lax.slice_in_dim(grad_hidden, 0, lax.axi...  53.6 us
    ppermute x2, waiting for transfers between devices, passed_along(): return lax.ppermute(value, axis, pairs)  36.6 us
    psum x1, blocking collectives, per_device(): lax.psum((gain_local[None], squares), ('dp', 'tensor'))  33.2 us
    all_gather x1, waiting for transfers between devices, per_device(): rows_kept = lax.all_gather(normed_one, 'tensor', axis=0, tiled=True)  31.3 us
    all_gather x1, waiting for transfers between devices, per_device(): rows_all = lax.all_gather(normed_two, 'tensor', axis=0, tiled=True)  29.1 us
  transfers between devices with their start and end apart: 11, of which 11 were waited for; matrix products, arithmetic and copies ran while one was open for 2% of the time, Pallas kernels for 0%

commit v1 on v0

v1 whole, which is shorter than its diff:
```python
from types import SimpleNamespace

import jax
import jax.numpy as jnp
from jax import lax
from jax.experimental import pallas as pl
from jax.experimental.pallas import tpu as pltpu
from jax.sharding import PartitionSpec as P

HS = 64
EPSILON = 1e-05
MASKED = -1e30
BF = jnp.bfloat16
F32 = jnp.float32
MESH = pl.DeviceIdType.MESH
PIECE = 96
ROOT = 0.7978845608028654


def dot_nn(a, b):
    return jnp.dot(a, b, preferred_element_type=F32)


def dot_nt(a, b):
    return lax.dot_general(a, b, (((1,), (1,)), ((), ())), preferred_element_type=F32)


def dot_tn(a, b):
    return lax.dot_general(a, b, (((0,), (0,)), ((), ())), preferred_element_type=F32)


def rows(start, count, multiple):
    return pl.ds(pl.multiple_of(start, multiple), count)


def lane_groups(value):
    return [value[:, i : i + 128] for i in range(0, value.shape[1], 128)]


def kernel_for(sizes):
    R, H, D, C, FF, NH, N = (sizes[k] for k in ("R", "H", "D", "C", "FF", "NH", "N"))
    QW = NH * 3 * HS
    AW = NH * HS
    PIECES = (2 * D + AW + QW) // PIECE
    DOWN, UP, OUT, QKV = 0, FF, FF + D, FF + D + AW
    half_n = N // 2

    names = {}

    def scratch(name, shape, dtype):
        names[name] = pltpu.VMEM(shape, dtype)

    scratch("gbuf", (2, 8, D), F32)
    scratch("sp", (R, D), BF)
    scratch("wao", (AW, D), BF)
    scratch("wdn", (FF, D), BF)
    scratch("n1", (4 * R, D), BF)
    scratch("q", (NH, 4 * R, HS), BF)
    scratch("k", (NH, 4 * R, HS), BF)
    scratch("v", (NH, 4 * R, HS), BF)
    scratch("e", (10 * NH, H, R), BF)
    scratch("il", (NH, 4 * H, 1), F32)
    scratch("att", (4 * H, AW), BF)
    scratch("proj", (4, H, D), BF)
    scratch("rsc", (2, H, D), BF)
    scratch("ysnd", (H, D), BF)
    scratch("rsy", (H, D), BF)
    scratch("mid", (H, D), BF)
    scratch("n2", (4 * H, D), BF)
    scratch("cot", (4 * H, D), BF)
    scratch("act", (4 * H, FF), BF)
    scratch("gh", (4 * H, FF), BF)
    scratch("gp", (4, H, D), BF)
    scratch("rsc2", (2, H, D), BF)
    scratch("ysnd2", (H, D), BF)
    scratch("rsy2", (H, D), BF)
    scratch("gm", (4 * H, D), BF)
    scratch("gother", (H, D), BF)
    scratch("dmt", (QW, R), BF)
    scratch("dkt", (4, NH, HS, R), F32)
    scratch("dvt", (4, NH, HS, R), F32)
    scratch("gq", (QW, D), F32)
    scratch("rscf", (2, R, D), BF)
    scratch("rsyf", (R, D), BF)
    scratch("rsxf", (R, D), BF)
    scratch("gsrc", (PIECES * PIECE, D), BF)
    scratch("gb", (PIECES * PIECE // 2, D), BF)
    scratch("gc", (PIECES * PIECE // 2, D), BF)
    scratch("sm", (5, 8, D), F32)
    scratch("smr", (3, 8, D), F32)
    scratch("smz", (N, 8, D), F32)
    n_vmem = len(names)
    S_SRC, S_PART, S_OUT = 0, PIECES, 2 * PIECES
    R_A, R_B, R_C, R_RES = 0, PIECES, 2 * PIECES, 3 * PIECES
    FIRST = 4 * PIECES
    N_SEM = FIRST + 64 + N
    scratch_shapes = list(names.values()) + [
        pltpu.SemaphoreType.DMA((N_SEM,)),
        pltpu.SemaphoreType.DMA((N_SEM,)),
    ]

    def body(
        lens, gains, stream, cot_in, w_qkv, w_ao, w_up, w_dn, o_io, o_gr, o_sm, *refs
    ):
        m = SimpleNamespace(**dict(zip(names, refs[:n_vmem], strict=True)))
        ssem, rsem = refs[n_vmem:]
        res = o_gr
        x = lax.axis_index("blk")
        d = lax.axis_index("dp")
        t = lax.axis_index("tensor")
        y = lax.div(t, 2)
        c = lax.rem(t, 2)
        t1 = 2 * y + 1 - c
        t2 = 2 * (1 - y) + c
        t3 = 2 * (1 - y) + 1 - c
        core, ydev, xdev = (x, d, t1), (x, d, t2), (1 - x, d, t)
        xh, oh = x * H, (1 - x) * H

        counter = [FIRST]
        pending = []

        def link(src, dst, dev, s_idx=None, r_idx=None):
            if s_idx is None:
                s_idx = r_idx = counter[0]
                counter[0] += 1
            return pltpu.make_async_remote_copy(
                src_ref=src,
                dst_ref=dst,
                send_sem=ssem.at[s_idx],
                recv_sem=rsem.at[r_idx],
                device_id=dev,
                device_id_type=MESH,
            )

        def send(src, dst, dev):
            copy = link(src, dst, dev)
            copy.start()
            pending.append(copy)
            return copy

        barrier = pltpu.get_barrier_semaphore()
        for peer in (core, ydev, xdev):
            pl.semaphore_signal(barrier, inc=1, device_id=peer, device_id_type=MESH)
        for j in range(1, N):
            pl.semaphore_signal(
                barrier,
                inc=1,
                device_id=(x, lax.rem(d + j, N), t),
                device_id_type=MESH,
            )
        pl.semaphore_wait(barrier, 3 + N - 1)

        lane = lax.broadcasted_iota(jnp.int32, (1, D), 1)
        last = lane == D - 1

        def total(value):
            return jnp.sum(value, axis=1, keepdims=True)

        def full_of(stream_rows):
            full = jnp.where(last, -total(stream_rows), stream_rows)
            return full, lax.rsqrt(total(full * full) * (1.0 / D) + EPSILON)

        def crms_back(grad, full, r, gain):
            a = grad * gain
            mean = total(a * full) * (1.0 / D)
            df = r * (a - full * (r * r * mean))
            tail = total(jnp.where(last, df, 0.0))
            return jnp.where(last, 0.0, df - tail)

        m.gbuf[x] = jnp.broadcast_to(gains[...], (8, D))
        gain_copy = send(m.gbuf.at[x], m.gbuf.at[x], xdev)
        m.sp[:, D - 128 :] = jnp.zeros((R, 128), BF)
        m.sp[:, :C] = stream[...]
        m.wao[:, D - 128 :] = jnp.zeros((AW, 128), BF)
        m.wao[:, :C] = w_ao[...]
        m.wdn[:, D - 128 :] = jnp.zeros((FF, 128), BF)
        m.wdn[:, :C] = w_dn[...]
        here = rows(t * H, H, H)
        m.cot[here, D - 128 :] = jnp.zeros((H, 128), BF)
        m.cot[here, :C] = cot_in[rows(xh, H, H), :]
        gain_copy.wait_recv()

        def norm_one(start, count):
            def step(i, _):
                r0 = start + i * 64
                full, r = full_of(m.sp[rows(r0, 64, 64), :].astype(F32))
                m.n1[rows(t * R + r0, 64, 64), :] = (full * r * m.gbuf[0, :1, :]).astype(BF)
                return 0

            lax.fori_loop(0, count // 64, step, 0)

        half = H // 2
        norm_one(xh, H)
        y_copies = []
        for k in range(2):
            part = m.n1.at[rows(t * R + xh + k * half, half, half)]
            y_copies.append(send(part, part, ydev))
        norm_one(oh, H)
        part = m.n1.at[rows(t * R, R, R)]
        own_copy = send(part, part, core)
        part = m.cot.at[here]
        cot_core = send(part, part, core)

        def qkv_rows(start):
            mixed = dot_nn(m.n1[rows(start, H, H), :], w_qkv[...])
            at = rows(start, H, H)
            for h in range(NH):
                for p, ref in enumerate((m.q, m.k, m.v)):
                    part = mixed[:, (3 * h + p) * HS : (3 * h + p + 1) * HS]
                    if p == 0:
                        part = part * HS**-0.5
                    ref[h, at, :] = part.astype(BF)

        def qkv_block(block):
            lax.fori_loop(0, 2, lambda i, _: (qkv_rows(block * R + i * H), 0)[1], 0)

        qkv_block(t)
        own_copy.wait_recv()
        qkv_block(t1)
        fwd = []
        x_copies = []
        for k in range(2):
            y_copies[k].wait_recv()
            part = m.n1.at[rows(t2 * R + xh + k * half, half, half)]
            x_copies.append(send(part, part, xdev))
            fwd.append(send(part, part, core))
        part = m.cot.at[here]
        cot_y = send(part, part, ydev)
        for k in range(2):
            x_copies[k].wait_recv()
            part = m.n1.at[rows(t2 * R + oh + k * half, half, half)]
            fwd.append(send(part, part, core))
        qkv_block(t2)
        for copy in fwd:
            copy.wait_recv()
        qkv_block(t3)

        ends = [lens[0]]
        for i in range(1, 4):
            ends.append(ends[-1] + lens[i])

        def bias_of(b, kb):
            cut = (ends[0] > kb * R) & (ends[0] <= b * R)
            for e in ends[1:]:
                cut = cut | ((e > kb * R) & (e <= b * R))
            return jnp.where(cut, MASKED, 0.0).astype(F32)

        row_at = lax.broadcasted_iota(jnp.int32, (H, R), 0)
        col_at = lax.broadcasted_iota(jnp.int32, (H, R), 1)

        def unit(b, kb):
            return lax.div(b * (b + 1), 2) + kb

        def attend(b):
            mine = rows(b * R + xh, H, H)
            heads = [m.q[h, mine, :] for h in range(NH)]

            def scores(h, kb):
                return dot_nt(heads[h], m.k[h, rows(kb * R, R, R), :])

            def top(s, best):
                for g in lane_groups(s):
                    best = jnp.maximum(best, g)
                return best

            def masked(s):
                return jnp.where(col_at <= row_at + xh, s, MASKED)

            def peak(kb, best):
                bias = bias_of(b, kb)
                return tuple(top(scores(h, kb) + bias, best[h]) for h in range(NH))

            low = jnp.full((H, 128), MASKED, F32)
            best = tuple(top(masked(scores(h, b)), low) for h in range(NH))
            best = lax.fori_loop(0, b, peak, best)
            best = [jnp.max(v, axis=1, keepdims=True) for v in best]

            def weigh(h, kb, s, sums, acc):
                e = jnp.exp(s - best[h])
                for g in lane_groups(e):
                    sums = sums + g
                e = e.astype(BF)
                m.e[unit(b, kb) * NH + h] = e
                return sums, acc + dot_nn(e, m.v[h, rows(kb * R, R, R), :])

            def add(kb, carry):
                bias = bias_of(b, kb)
                return tuple(weigh(h, kb, scores(h, kb) + bias, *carry[h]) for h in range(NH))

            zero = (jnp.zeros((H, 128), F32), jnp.zeros((H, HS), F32))
            carry = tuple(weigh(h, b, masked(scores(h, b)), *zero) for h in range(NH))
            carry = lax.fori_loop(0, b, add, carry)
            at = rows(b * H, H, H)
            for h in range(NH):
                inverse = 1.0 / total(carry[h][0])
                m.il[h, at, :] = inverse
                m.att[at, h * HS : (h + 1) * HS] = (carry[h][1] * inverse).astype(BF)
            return dot_nn(m.att[at, :], m.wao[...]).astype(BF)

        C_PROJ = counter[0]
        counter[0] += 2

        def proj_copy(i):
            j = lax.div(i, 2)
            return link(m.proj.at[i], m.rsc.at[j], core, C_PROJ + j, C_PROJ + j)

        def add_rows(out, terms, count):
            def step(i, _):
                at = rows(i * 64, 64, 64)
                out[at, :] = sum(ref[at, :].astype(F32) for ref in terms).astype(BF)
                return 0

            lax.fori_loop(0, count // 64, step, 0)

        y_proj = link(m.ysnd, m.rsy, ydev)
        pending.append(y_proj)

        def attend_step(i, _):
            a, e = lax.div(i, 2), 1 - lax.rem(i, 2)
            g = (1 - y) * (1 - a) + y * a
            m.proj[i] = attend(2 * g + e)

            @pl.when(lax.rem(i, 2) == c)
            def _():
                proj_copy(i).start()

            @pl.when(i == 2)
            def _():
                proj_copy(c).wait_recv()
                add_rows(m.ysnd, (m.proj.at[1 - c], m.rsc.at[0]), H)
                y_proj.start()

            return 0

        lax.fori_loop(0, 4, attend_step, 0)
        proj_copy(2 + c).wait_recv()
        cot_core.wait_recv()
        cot_y.wait_recv()
        part = m.cot.at[rows(t2 * H, H, H)]
        cot_fwd = send(part, part, core)
        y_proj.wait_recv()

        def middle_step(i, squares):
            at = rows(i * 64, 64, 64)
            mid = m.sp[rows(xh + i * 64, 64, 64), :].astype(F32)
            mid = mid + m.proj[2 + 1 - c, at, :].astype(F32)
            mid = mid + m.rsc[1, at, :].astype(F32) + m.rsy[at, :].astype(F32)
            mid = mid.astype(BF)
            m.mid[at, :] = mid
            full, r = full_of(mid.astype(F32))
            m.n2[rows(t * H + i * 64, 64, 64), :] = (full * r * m.gbuf[1, :1, :]).astype(BF)
            return squares + jnp.sum(full * full, axis=0, keepdims=True)

        squares = lax.fori_loop(0, H // 64, middle_step, jnp.zeros((1, D), F32))
        m.sm[0] = jnp.zeros((8, D), F32)
        m.sm[0, 2:3, :] = squares

        n2_y = send(m.n2.at[here], m.n2.at[here], ydev)
        n2_core = send(m.n2.at[here], m.n2.at[here], core)

        def feed(s, i):
            at = rows(s * H, H, H)
            for f in range(FF // 256):
                cols = slice(f * 256, (f + 1) * 256)
                hidden = dot_nn(m.n2[at, :], w_up[:, cols])
                grad = dot_nt(m.cot[at, :], m.wdn[cols, :])
                square = hidden * hidden
                bent = jnp.tanh(ROOT * hidden * (1.0 + 0.044715 * square))
                gate = 0.5 * (1.0 + bent)
                m.act[at, cols] = (hidden * gate).astype(BF)
                slope = gate + (0.5 * ROOT) * hidden * (1.0 - bent * bent) * (
                    1.0 + (3 * 0.044715) * square
                )
                m.gh[at, cols] = (grad * slope).astype(BF)
            m.gp[i] = dot_nt(m.gh[at, :], w_up[...]).astype(BF)

        C_GP = counter[0]
        counter[0] += 2
        C_N2 = counter[0]
        counter[0] += 1
        gp_copies = [
            link(m.gp.at[2 * j + 1], m.rsc2.at[j], core, C_GP + j, C_GP + j) for j in range(2)
        ]
        part = m.n2.at[rows(t2 * H, H, H)]
        n2_fwd = link(part, part, core, C_N2, C_N2)
        pending.append(n2_fwd)
        pending.extend(gp_copies)

        def feed_step(i, _):
            a, e = lax.div(i, 2), lax.rem(i, 2)
            s = 2 * (y + a - 2 * y * a) + (c + e - 2 * c * e)

            @pl.when(i == 1)
            def _():
                n2_core.wait_recv()

            @pl.when(i == 2)
            def _():
                n2_y.wait_recv()
                n2_fwd.start()
                cot_fwd.wait_recv()

            @pl.when(i == 3)
            def _():
                n2_fwd.wait_recv()

            feed(s, i)

            @pl.when(i == 1)
            def _():
                gp_copies[0].start()

            @pl.when(i == 3)
            def _():
                gp_copies[1].start()

            return 0

        lax.fori_loop(0, 4, feed_step, 0)
        gp_copies[1].wait_recv()
        add_rows(m.ysnd2, (m.gp.at[2], m.rsc2.at[1]), H)
        gp_y = send(m.ysnd2, m.rsy2, ydev)

        is_mid = (d == half_n - 1) | (d == half_n)
        is_end = (d == 0) | (d == N - 1)
        side = jnp.where(d < half_n, 0, 1)
        step_in = 1 - 2 * side
        inner = (x, lax.rem(d + step_in + N, N), t)
        outer = (x, lax.rem(d - step_in + N, N), t)

        def piece(ref, p):
            return ref.at[rows(p * PIECE, PIECE, 16)]

        def in_copy(p):
            return link(piece(m.gsrc, p), piece(res, p), inner, S_SRC + p, R_A + p)

        def mid_copy(p):
            to = piece(m.gb, lax.div(p, 2))
            return link(piece(m.gsrc, p), to, inner, S_SRC + p, R_B + p)

        def x_copy(p):
            to = piece(m.gc, lax.div(p, 2))
            return link(piece(m.gsrc, p), to, xdev, S_SRC + p, R_C + p)

        def part_copy(p):
            return link(piece(res, p), piece(res, p), inner, S_PART + p, R_RES + p)

        def out_copy(p):
            return link(piece(res, p), piece(res, p), outer, S_OUT + p, R_RES + p)

        def gather_piece(out, p, ref, q):
            def step(i, _):
                at = rows(p * PIECE + i * 32, 32, 16)
                other = ref[rows(q * PIECE + i * 32, 32, 16), :].astype(F32)
                out[at, :] = (m.gsrc[at, :].astype(F32) + other).astype(BF)
                return 0

            lax.fori_loop(0, PIECE // 32, step, 0)

        def valid(p):
            return (p >= 0) & (p < PIECES)

        def owns(p):
            return is_mid & (side == lax.rem(p + 2 * PIECES, 2))

        def serve(s):
            @pl.when(valid(s) & jnp.logical_not(is_mid))
            def _():
                if N > 4:

                    @pl.when(jnp.logical_not(is_end))
                    def _():
                        in_copy(s).wait_recv()
                        gather_piece(m.gsrc, s, res, s)

                in_copy(s).start()

            p2 = s - 1

            @pl.when(valid(p2) & is_mid)
            def _():
                @pl.when(jnp.logical_not(is_end))
                def _():
                    in_copy(p2).wait_recv()
                    gather_piece(m.gsrc, p2, res, p2)

                @pl.when(jnp.logical_not(owns(p2)))
                def _():
                    mid_copy(p2).start()

            p3 = s - 2

            @pl.when(valid(p3) & owns(p3))
            def _():
                mid_copy(p3).wait_recv()
                gather_piece(m.gsrc, p3, m.gb, lax.div(p3, 2))
                x_copy(p3).start()

            p4 = s - 3

            @pl.when(valid(p4) & owns(p4))
            def _():
                x_copy(p4).wait_recv()
                gather_piece(res, p4, m.gc, lax.div(p4, 2))
                part_copy(p4).start()

                @pl.when(jnp.logical_not(is_end))
                def _():
                    out_copy(p4).start()

            p5 = s - 4

            @pl.when(valid(p5) & is_mid & jnp.logical_not(owns(p5)))
            def _():
                part_copy(p5).wait_recv()

                @pl.when(jnp.logical_not(is_end))
                def _():
                    out_copy(p5).start()

            if N > 4:
                p6 = s - 5

                @pl.when(valid(p6) & jnp.logical_not(is_mid) & jnp.logical_not(is_end))
                def _():
                    part_copy(p6).wait_recv()
                    out_copy(p6).start()

        def serve_all_sent():
            def step(p, _):
                @pl.when(is_end & jnp.logical_not(is_mid))
                def _():
                    part_copy(p).wait_recv()

                in_copy(p).wait_send()

                @pl.when(owns(p))
                def _():
                    part_copy(p).wait_send()

                @pl.when(jnp.logical_not(is_end))
                def _():
                    out_copy(p).wait_send()

                return 0

            lax.fori_loop(0, PIECES, step, 0)

        def down_step(f, _):
            at = pl.ds(pl.multiple_of(f * 256, 256), 256)
            m.gsrc[rows(DOWN + f * 256, 256, 16), :] = dot_tn(m.act[:, at], m.cot[...]).astype(BF)
            return 0

        def up_step(f, _):
            at = pl.ds(pl.multiple_of(f * 256, 256), 256)
            m.gsrc[rows(UP + f * 256, 256, 16), :] = dot_tn(m.n2[:, at], m.gh[...]).astype(BF)
            return 0

        lax.fori_loop(0, FF // 256, down_step, 0)
        serve(0)

        gp_copies[0].wait_recv()
        gp_y.wait_recv()

        def grad_middle_step(i, gain):
            at = rows(i * 64, 64, 64)
            grad = m.gp[0, at, :].astype(F32) + m.rsc2[0, at, :].astype(F32)
            grad = grad + m.rsy2[at, :].astype(F32)
            full, r = full_of(m.mid[at, :].astype(F32))
            back = crms_back(grad, full, r, m.gbuf[1, :1, :])
            mine = rows(t * H + i * 64, 64, 64)
            m.gm[mine, :] = (m.cot[mine, :].astype(F32) + back).astype(BF)
            return gain + jnp.sum(grad * full * r, axis=0, keepdims=True)

        gain_two = lax.fori_loop(0, H // 64, grad_middle_step, jnp.zeros((1, D), F32))
        m.sm[0, 1:2, :] = gain_two
        gm_y = send(m.gm.at[here], m.gm.at[here], ydev)
        gm_core = send(m.gm.at[here], m.gm.at[here], core)
        gm_x = link(m.gm.at[here], m.gother, xdev)

        @pl.when(x == 1)
        def _():
            gm_x.start()

        lax.fori_loop(0, D // 256, up_step, 0)
        serve(1)

        def mlp_step(i, _):
            a, e = lax.div(i, 2), lax.rem(i, 2)
            s = 2 * (y + a - 2 * y * a) + (c + e - 2 * c * e)
            m.proj[i] = dot_nn(m.act[rows(s * H, H, H), :], m.wdn[...]).astype(BF)
            return 0

        proj_copy(c).wait_send()
        proj_copy(2 + c).wait_send()
        lax.fori_loop(0, 4, mlp_step, 0)
        mp_copies = [send(m.proj.at[2 * j + 1], m.rsc.at[j], core) for j in range(2)]
        serve(2)
        gm_y.wait_recv()
        part = m.gm.at[rows(t2 * H, H, H)]
        gm_fwd = send(part, part, core)
        mp_copies[1].wait_recv()
        y_proj.wait_send()
        add_rows(m.ysnd, (m.proj.at[2], m.rsc.at[1]), H)
        mp_y = send(m.ysnd, m.rsy, ydev)
        gm_core.wait_recv()
        gm_fwd.wait_recv()

        m.gsrc[OUT : OUT + AW, :] = dot_tn(m.att[...], m.gm[...]).astype(BF)
        m.dkt[...] = jnp.zeros_like(m.dkt)
        m.dvt[...] = jnp.zeros_like(m.dvt)
        m.gq[...] = jnp.zeros_like(m.gq)

        C_GN = counter[0]
        counter[0] += 2

        def pair_rows(j):
            return rows(j * R, R, R)

        def gn_copy(j):
            return link(m.gh.at[pair_rows(j)], m.rscf.at[j], core, C_GN + j, C_GN + j)

        C_YF = counter[0]
        counter[0] += 4
        chunk = R // 4

        def yf_copy(k):
            src = m.act.at[rows((1 - y) * R + k * chunk, chunk, chunk)]
            dst = m.rsyf.at[rows(k * chunk, chunk, chunk)]
            return link(src, dst, ydev, C_YF + k, C_YF + k)

        def send_far():
            gn_copy(1 - y).wait_recv()

            def step(k, _):
                def inside(i, _):
                    r0 = k * chunk + i * 64
                    at = rows((1 - y) * R + r0, 64, 64)
                    both = m.act[at, :].astype(F32) + m.rscf[1 - y, rows(r0, 64, 64), :].astype(F32)
                    m.act[at, :] = both.astype(BF)
                    return 0

                lax.fori_loop(0, chunk // 64, inside, 0)
                yf_copy(k).start()
                return 0

            lax.fori_loop(0, 4, step, 0)

        far_step = 3 - (2 * (1 - y) + c)

        def back_block(i, _):
            b = 3 - i
            at = rows(b * H, H, H)
            mine = rows(b * R + xh, H, H)
            grad_att = dot_nt(m.gm[at, :], m.wao[...])
            outs, offs, out_ts, q_ts = [], [], [], []
            for h in range(NH):
                cols = slice(h * HS, (h + 1) * HS)
                inverse = m.il[h, at, :]
                out = grad_att[:, cols].astype(BF).astype(F32)
                delta = total(out * m.att[at, cols].astype(F32))
                offs.append(delta * inverse)
                out = (out * inverse).astype(BF)
                outs.append(out)
                out_ts.append(jnp.transpose(out))
                q_ts.append(jnp.transpose(m.q[h, mine, :]))

            def keys(kb, grads):
                new = []
                for h in range(NH):
                    e = m.e[unit(b, kb) * NH + h]
                    at_k = rows(kb * R, R, R)
                    dp = dot_nt(outs[h], m.v[h, at_k, :])
                    ds = (e.astype(F32) * (dp - offs[h])).astype(BF)
                    new.append(grads[h] + dot_nn(ds, m.k[h, at_k, :]))
                    m.dkt[kb, h] += dot_nn(q_ts[h], ds)
                    m.dvt[kb, h] += dot_nn(out_ts[h], e)
                serve(3 + 4 * i - lax.div(i * (i - 1), 2) + kb)
                return tuple(new)

            grads = lax.fori_loop(0, b + 1, keys, (jnp.zeros((H, HS), F32),) * NH)
            for h in range(NH):
                base = 3 * h * HS
                grad_q = jnp.transpose(grads[h] * HS**-0.5).astype(BF)
                m.dmt[base : base + HS, rows(xh, H, H)] = grad_q
                m.dmt[base : base + HS, rows(oh, H, H)] = jnp.zeros((HS, H), BF)
                m.dmt[base + HS : base + 2 * HS, :] = m.dkt[b, h].astype(BF)
                m.dmt[base + 2 * HS : base + 3 * HS, :] = m.dvt[b, h].astype(BF)
            n1_rows = rows(b * R, R, R)
            m.gq[...] += dot_nn(m.dmt[...], m.n1[n1_rows, :])
            back = dot_nt(jnp.transpose(m.dmt[...]), w_qkv[...]).astype(BF)
            j = lax.div(b, 2)

            @pl.when(lax.rem(b, 2) == c)
            def _():
                m.act[pair_rows(j), :] = back

            @pl.when(lax.rem(b, 2) != c)
            def _():
                m.gh[pair_rows(j), :] = back
                gn_copy(j).start()

            @pl.when(i == far_step + 1)
            def _():
                send_far()

            return 0

        lax.fori_loop(0, 4, back_block, 0)
        pl.when(far_step == 3)(send_far)
        m.gsrc[QKV : QKV + QW, :] = m.gq[...].astype(BF)
        served = 13

        mp_copies[0].wait_recv()
        mp_y.wait_recv()
        n2_y.wait_send()
        n2_core.wait_send()
        add_rows(m.n2.at[here], (m.mid, m.proj.at[0], m.rsc.at[0], m.rsy), H)
        bo_x = link(m.n2.at[here], m.gother, xdev)

        @pl.when(x == 0)
        def _():
            bo_x.start()

        lax.fori_loop(served, 18, lambda s, _: (serve(s), 0)[1], 0)

        gn_copy(y).wait_recv()

        C_XF = counter[0]
        counter[0] += 4

        def xf_copy(k):
            src = m.act.at[rows(y * R + k * chunk, chunk, chunk)]
            dst = m.rsxf.at[rows(k * chunk, chunk, chunk)]
            return link(src, dst, xdev, C_XF + k, C_XF + k)

        def near_sum(k):
            yf_copy(k).wait_recv()

            def inside(i, _):
                r0 = k * chunk + i * 64
                at = rows(y * R + r0, 64, 64)
                here_rows = rows(r0, 64, 64)
                both = m.act[at, :].astype(F32) + m.rscf[y, here_rows, :].astype(F32)
                m.act[at, :] = (both + m.rsyf[here_rows, :].astype(F32)).astype(BF)
                return 0

            lax.fori_loop(0, chunk // 64, inside, 0)

        @pl.when(x == 1)
        def _():
            def step(k, _):
                near_sum(k)
                xf_copy(k).start()
                return 0

            lax.fori_loop(0, 4, step, 0)

        @pl.when(x == 0)
        def _():
            gm_x.wait_recv()
            m.sm[0, 0:1, :] = jnp.zeros((1, D), F32)

            def step(k, _):
                near_sum(k)
                xf_copy(k).wait_recv()

                def inside(i, gain):
                    r0 = k * chunk + i * 64
                    here_rows = rows(r0, 64, 64)
                    grad = m.act[rows(y * R + r0, 64, 64), :].astype(F32)
                    grad = grad + m.rsxf[here_rows, :].astype(F32)
                    full, r = full_of(m.sp[here_rows, :].astype(F32))
                    back = crms_back(grad, full, r, m.gbuf[0, :1, :])
                    m.rsyf[here_rows, :] = back.astype(BF)
                    return gain + jnp.sum(grad * full * r, axis=0, keepdims=True)

                gain = lax.fori_loop(0, chunk // 64, inside, jnp.zeros((1, D), F32))
                m.sm[0, 0:1, :] += gain
                return 0

            lax.fori_loop(0, 4, step, 0)

            def out_step(i, _):
                at = rows(i * 64, 64, 64)
                one = m.gm[rows(t * H + i * 64, 64, 64), :].astype(F32) + m.rsyf[at, :].astype(F32)
                o_io[0, at, :] = one[:, :C].astype(BF)
                below = rows(H + i * 64, 64, 64)
                two = m.gother[at, :].astype(F32) + m.rsyf[below, :].astype(F32)
                o_io[0, below, :] = two[:, :C].astype(BF)
                return 0

            lax.fori_loop(0, H // 64, out_step, 0)

        @pl.when(x == 1)
        def _():
            bo_x.wait_recv()
            o_io[0, 0:H, :] = m.gother[:, :C]
            o_io[0, H:R, :] = m.n2[here, :C]

        for j, peer in enumerate((core, ydev, xdev)):
            copy = send(m.sm.at[j], m.smr.at[j], peer)
            copy.wait_recv()
            m.sm[j + 1] = m.sm[j] + m.smr[j]
        z_copies = []
        for j in range(1, N):
            z_copies.append(send(m.sm.at[3], m.smz.at[j], (x, lax.rem(d + j, N), t)))
        lax.fori_loop(18, PIECES + 6, lambda s, _: (serve(s), 0)[1], 0)
        everything = m.sm[3]
        for j in range(1, N):
            z_copies[j - 1].wait_recv()
            everything = everything + m.smz[j]
        o_sm[...] = everything

        serve_all_sent()
        waited = {id(n2_y), id(n2_core), id(y_proj)}
        for copy in pending:
            if id(copy) not in waited:
                copy.wait_send()
        for j in range(2):
            gn_copy(j).wait_send()
        for k in range(4):
            yf_copy(k).wait_send()

        @pl.when(x == 1)
        def _():
            gm_x.wait_send()
            for k in range(4):
                xf_copy(k).wait_send()

        @pl.when(x == 0)
        def _():
            bo_x.wait_send()

        assert counter[0] <= N_SEM

    return body, scratch_shapes, PIECES * PIECE, (DOWN, UP, OUT, QKV)


def per_device(mesh):
    N = mesh.shape["dp"]
    assert mesh.shape["blk"] == 2 and mesh.shape["tensor"] == 4 and N % 2 == 0

    def run(stream_in, lengths, norm_gains, w_qkv, w_attn_out, w_up, w_down, cotangent):
        R, C = stream_in.shape
        D = norm_gains.shape[1]
        FF = w_up.shape[1]
        NH = w_qkv.shape[1] // (3 * HS)
        body, scratch, grad_rows, (DOWN, UP, OUT, QKV) = kernel_for(
            dict(R=R, H=R // 2, D=D, C=C, FF=FF, NH=NH, N=N)
        )
        vmem = pl.BlockSpec(memory_space=pltpu.VMEM)
        block_io, grads, small = pl.pallas_call(
            body,
            out_shape=(
                jax.ShapeDtypeStruct((1, R, C), BF),
                jax.ShapeDtypeStruct((grad_rows, D), BF),
                jax.ShapeDtypeStruct((8, D), F32),
            ),
            in_specs=[pl.BlockSpec(memory_space=pltpu.SMEM)] + [vmem] * 7,
            out_specs=(vmem,) * 3,
            scratch_shapes=scratch,
            compiler_params=pltpu.CompilerParams(
                collective_id=0, has_side_effects=True, vmem_limit_bytes=62 << 20
            ),
        )(lengths, norm_gains, stream_in, cotangent, w_qkv, w_attn_out, w_up, w_down)
        gain = jnp.where(lax.axis_index("blk") == 0, small[0:1], small[1:2])
        entries = 4 * R * N * D
        stream_rms = jnp.sqrt(jnp.sum(small[2]) / entries)
        return (
            block_io,
            gain,
            grads[QKV:].T.astype(F32),
            grads[OUT:QKV, :C].astype(F32),
            grads[UP:OUT].astype(F32),
            grads[DOWN:UP, :C].astype(F32),
            stream_rms,
        )

    return run


def solution(mesh):
    in_specs = (
        P(("dp", "tensor"), None),
        P("dp"),
        P("blk", None),
        P(None, "tensor"),
        P("tensor", None),
        P(None, "tensor"),
        P("tensor", None),
        P(("dp", "tensor"), None),
    )
    out_specs = (
        P("blk", ("dp", "tensor"), None),
        P("blk", None),
        P(None, "tensor"),
        P("tensor", None),
        P(None, "tensor"),
        P("tensor", None),
        P(),
    )
    return jax.shard_map(
        per_device(mesh), mesh=mesh, in_specs=in_specs, out_specs=out_specs, check_vma=False
    )
```

time: 883 us -> 249 us (0.28)
  waiting for transfers between devices: 623 us -> 0 us
  Pallas kernels: 0 us -> 234 us
  matrix products: 93.6 us -> 0 us
  loops' own time: 35.2 us -> 0 us
  blocking collectives: 33.2 us -> 0 us
  local copies, waits for them, and re-layouts: 33.9 us -> 3.11 us
  other arithmetic: 37 us -> 9.58 us
  between operations: 17.5 us -> 2.48 us
    psum x1 -> x0, waiting for transfers between devices: 238 us -> none  [per_device(): lax.psum((grad_qkv, grad_out_w, grad_up, grad_down), ('blk', 'dp'))]
    reduce_scatter x4 -> x0, waiting for transfers between devices: 234 us -> none  [the longest x1 93.1 us: per_device(): lax.psum_scatter(times_transpose(grad_mixed, w_qkv).astype(jnp.bfloat16),...]
    pallas_call x0 -> x1, Pallas kernels: none -> 234 us  [run(): pl.pallas_call(body, out_shape=(jax.ShapeDtypeStruct((1, R, C), BF), jax....]
    all_gather x4 -> x0, waiting for transfers between devices: 113 us -> none  [the longest x1 31.3 us: per_device(): rows_kept = lax.all_gather(normed_one, 'tensor', axis=0, tiled=True)]
    dot_general x36 -> x0, matrix products: 93.6 us -> none  [the longest x8 16.6 us: window_scores(): jnp.einsum('qhe,khe->hqk', query_rows, key_rows, preferred_element_type=j...]
    ppermute x2 -> x0, waiting for transfers between devices: 36.6 us -> none  [passed_along(): return lax.ppermute(value, axis, pairs)]
    another operation x14 -> x0, loops' own time: 35.2 us -> none  [the longest x1 28.2 us: attend_back(): lax.fori_loop(0, queries.shape[0] // SHORT, back_turn, (zeros_all, zeros_...]
    psum x1 -> x0, blocking collectives: 33.2 us -> none  [per_device(): lax.psum((gain_local[None], squares), ('dp', 'tensor'))]
  transfers between devices with their start and end apart: 11 -> 0, of which waited for: 11 -> 0; matrix products, arithmetic and copies ran while one was open for 2% -> 0% of each run, Pallas kernels for 0% -> 0%
where the time goes in v1:
time: 249 us
  Pallas kernels  234 us (94%)
  other arithmetic  9.58 us (4%)
  local copies, waits for them, and re-layouts  3.11 us (1%)
    pallas_call x1, Pallas kernels, run(): pl.pallas_call(body, out_shape=(jax.ShapeDtypeStruct((1, R, C), BF), jax....  234 us

profile of v1, /device:TPU:0, one launch (start us, length us, event | category | flops | bytes accessed | tf_op | source)
XLA Modules:
  0.0 248.8 jit_solution(14138544347392934256)
XLA Ops:
  0.6 2.2 copy.15.w_qkv
  2.9 233.6 %shard_map.135 = (bf16[1,512,767]{2,1,0:T(8,128)(2,1)}, bf16[2304,768]{1,0:T(8,128)(2,1)}, f32[8,768]{1,0:T(8,128)}) custom-call(s32[4]{0:T(128)} %lens.1, f32[1,768]{1,0:T(1,128)} %gains.1, bf16[512,767]{1,0:T(8,128)(2,1)} %stream.1, bf16[512,767]{1,0:T(8,128)(2,1)} %cot_in.1, bf16[768,576]{1,0:T(8,128)(2,1)} %copy.15.w_qkv, bf16[192,767]{1,0:T(8,128)(2,1)} %w_ao.1, ...), custom_call_target="tpu_custom_call" | custom-call | tf_op jit(solution)/shard_map/pallas_call | solution.py:853
  236.5 0.0 copy-start
  236.5 2.1 slice_reduce_fusion
  239.3 1.8 slice_convert_fusion.2
  241.1 2.5 %convert_bitcast_fusion = f32[768,576]{0,1:T(8,128)} fusion(bf16[2304,768]{1,0:T(8,128)(2,1)} %get-tuple-element.12), kind=kLoop, calls=%fused_computation | loop fusion | flops 442368 | bytes 2654208 | tf_op jit(solution)/shard_map/convert_element_type | solution.py:873
  243.6 0.0 copy-done
  243.6 1.6 slice_convert_fusion
  245.2 0.0 copy-start.1
  245.2 1.6 slice_convert_fusion.1
  246.7 0.0 copy-done.1
  246.8 0.9 copy.17
Async XLA Ops:
  236.5 7.1 %copy-start = (bf16[2304,768]{1,0:T(8,128)(2,1)S(1)}, bf16[2304,768]{1,0:T(8,128)(2,1)}, u32[]{:S(2)}) copy-start(bf16[2304,768]{1,0:T(8,128)(2,1)} %get-tuple-element.12) | copy-start | bytes 10616836
  245.2 1.6 copy-start.1

commit v2 on v1

--- a/solution.py
+++ b/solution.py
@@ -51,6 +51,12 @@
         names[name] = pltpu.VMEM(shape, dtype)
 
     scratch("gbuf", (2, 8, D), F32)
+    scratch("stream", (R, C), BF)
+    scratch("cot_in", (H, C), BF)
+    scratch("wqkv", (QW, D), BF)
+    scratch("wao_in", (AW, C), BF)
+    scratch("wup", (D, FF), BF)
+    scratch("wdn_in", (FF, C), BF)
     scratch("sp", (R, D), BF)
     scratch("wao", (AW, D), BF)
     scratch("wdn", (FF, D), BF)
@@ -97,13 +103,14 @@
     scratch_shapes = list(names.values()) + [
         pltpu.SemaphoreType.DMA((N_SEM,)),
         pltpu.SemaphoreType.DMA((N_SEM,)),
+        pltpu.SemaphoreType.DMA((6,)),
     ]
 
     def body(
         lens, gains, stream, cot_in, w_qkv, w_ao, w_up, w_dn, o_io, o_gr, o_sm, *refs
     ):
         m = SimpleNamespace(**dict(zip(names, refs[:n_vmem], strict=True)))
-        ssem, rsem = refs[n_vmem:]
+        ssem, rsem, lsem = refs[n_vmem:]
         res = o_gr
         x = lax.axis_index("blk")
         d = lax.axis_index("dp")
@@ -138,6 +145,20 @@
             pending.append(copy)
             return copy
 
+        loads = []
+        for i, (src, dst) in enumerate(
+            (
+                (stream, m.stream),
+                (w_qkv, m.wqkv),
+                (cot_in.at[rows(xh, H, H)], m.cot_in),
+                (w_ao, m.wao_in),
+                (w_up, m.wup),
+                (w_dn, m.wdn_in),
+            )
+        ):
+            loads.append(pltpu.make_async_copy(src, dst, lsem.at[i]))
+            loads[-1].start()
+
         barrier = pltpu.get_barrier_semaphore()
         for peer in (core, ydev, xdev):
             pl.semaphore_signal(barrier, inc=1, device_id=peer, device_id_type=MESH)
@@ -170,14 +191,9 @@
         m.gbuf[x] = jnp.broadcast_to(gains[...], (8, D))
         gain_copy = send(m.gbuf.at[x], m.gbuf.at[x], xdev)
         m.sp[:, D - 128 :] = jnp.zeros((R, 128), BF)
-        m.sp[:, :C] = stream[...]
-        m.wao[:, D - 128 :] = jnp.zeros((AW, 128), BF)
-        m.wao[:, :C] = w_ao[...]
-        m.wdn[:, D - 128 :] = jnp.zeros((FF, 128), BF)
-        m.wdn[:, :C] = w_dn[...]
+        loads[0].wait()
+        m.sp[:, :C] = m.stream[...]
         here = rows(t * H, H, H)
-        m.cot[here, D - 128 :] = jnp.zeros((H, 128), BF)
-        m.cot[here, :C] = cot_in[rows(xh, H, H), :]
         gain_copy.wait_recv()
 
         def norm_one(start, count):
@@ -189,20 +205,23 @@
 
             lax.fori_loop(0, count // 64, step, 0)
 
-        half = H // 2
-        norm_one(xh, H)
+        half = H // 4
         y_copies = []
-        for k in range(2):
+        for k in range(4):
+            norm_one(xh + k * half, half)
             part = m.n1.at[rows(t * R + xh + k * half, half, half)]
             y_copies.append(send(part, part, ydev))
         norm_one(oh, H)
         part = m.n1.at[rows(t * R, R, R)]
         own_copy = send(part, part, core)
+        loads[2].wait()
+        m.cot[here, D - 128 :] = jnp.zeros((H, 128), BF)
+        m.cot[here, :C] = m.cot_in[...]
         part = m.cot.at[here]
         cot_core = send(part, part, core)
 
         def qkv_rows(start):
-            mixed = dot_nn(m.n1[rows(start, H, H), :], w_qkv[...])
+            mixed = dot_nt(m.n1[rows(start, H, H), :], m.wqkv[...])
             at = rows(start, H, H)
             for h in range(NH):
                 for p, ref in enumerate((m.q, m.k, m.v)):
@@ -214,19 +233,26 @@
         def qkv_block(block):
             lax.fori_loop(0, 2, lambda i, _: (qkv_rows(block * R + i * H), 0)[1], 0)
 
+        loads[1].wait()
         qkv_block(t)
         own_copy.wait_recv()
         qkv_block(t1)
+        for load in loads[3:]:
+            load.wait()
+        m.wao[:, D - 128 :] = jnp.zeros((AW, 128), BF)
+        m.wao[:, :C] = m.wao_in[...]
+        m.wdn[:, D - 128 :] = jnp.zeros((FF, 128), BF)
+        m.wdn[:, :C] = m.wdn_in[...]
         fwd = []
         x_copies = []
-        for k in range(2):
+        for k in range(4):
             y_copies[k].wait_recv()
             part = m.n1.at[rows(t2 * R + xh + k * half, half, half)]
             x_copies.append(send(part, part, xdev))
             fwd.append(send(part, part, core))
         part = m.cot.at[here]
         cot_y = send(part, part, ydev)
-        for k in range(2):
+        for k in range(4):
             x_copies[k].wait_recv()
             part = m.n1.at[rows(t2 * R + oh + k * half, half, half)]
             fwd.append(send(part, part, core))
@@ -362,7 +388,7 @@
             at = rows(s * H, H, H)
             for f in range(FF // 256):
                 cols = slice(f * 256, (f + 1) * 256)
-                hidden = dot_nn(m.n2[at, :], w_up[:, cols])
+                hidden = dot_nn(m.n2[at, :], m.wup[:, cols])
                 grad = dot_nt(m.cot[at, :], m.wdn[cols, :])
                 square = hidden * hidden
                 bent = jnp.tanh(ROOT * hidden * (1.0 + 0.044715 * square))
@@ -372,7 +398,7 @@
                     1.0 + (3 * 0.044715) * square
                 )
                 m.gh[at, cols] = (grad * slope).astype(BF)
-            m.gp[i] = dot_nt(m.gh[at, :], w_up[...]).astype(BF)
+            m.gp[i] = dot_nt(m.gh[at, :], m.wup[...]).astype(BF)
 
         C_GP = counter[0]
         counter[0] += 2
@@ -475,7 +501,7 @@
 
                 in_copy(s).start()
 
-            p2 = s - 1
+            p2 = s - 2
 
             @pl.when(valid(p2) & is_mid)
             def _():
@@ -488,7 +514,7 @@
                 def _():
                     mid_copy(p2).start()
 
-            p3 = s - 2
+            p3 = s - 4
 
             @pl.when(valid(p3) & owns(p3))
             def _():
@@ -496,7 +522,7 @@
                 gather_piece(m.gsrc, p3, m.gb, lax.div(p3, 2))
                 x_copy(p3).start()
 
-            p4 = s - 3
+            p4 = s - 6
 
             @pl.when(valid(p4) & owns(p4))
             def _():
@@ -508,7 +534,7 @@
                 def _():
                     out_copy(p4).start()
 
-            p5 = s - 4
+            p5 = s - 8
 
             @pl.when(valid(p5) & is_mid & jnp.logical_not(owns(p5)))
             def _():
@@ -519,7 +545,7 @@
                     out_copy(p5).start()
 
             if N > 4:
-                p6 = s - 5
+                p6 = s - 10
 
                 @pl.when(valid(p6) & jnp.logical_not(is_mid) & jnp.logical_not(is_end))
                 def _():
@@ -688,7 +714,7 @@
                 m.dmt[base + 2 * HS : base + 3 * HS, :] = m.dvt[b, h].astype(BF)
             n1_rows = rows(b * R, R, R)
             m.gq[...] += dot_nn(m.dmt[...], m.n1[n1_rows, :])
-            back = dot_nt(jnp.transpose(m.dmt[...]), w_qkv[...]).astype(BF)
+            back = dot_nn(jnp.transpose(m.dmt[...]), m.wqkv[...]).astype(BF)
             j = lax.div(b, 2)
 
             @pl.when(lax.rem(b, 2) == c)
@@ -805,12 +831,24 @@
         z_copies = []
         for j in range(1, N):
             z_copies.append(send(m.sm.at[3], m.smz.at[j], (x, lax.rem(d + j, N), t)))
-        lax.fori_loop(18, PIECES + 6, lambda s, _: (serve(s), 0)[1], 0)
+        lax.fori_loop(18, PIECES + 12, lambda s, _: (serve(s), 0)[1], 0)
         everything = m.sm[3]
         for j in range(1, N):
             z_copies[j - 1].wait_recv()
             everything = everything + m.smz[j]
-        o_sm[...] = everything
+        o_sm[...] = jnp.zeros_like(o_sm)
+
+        @pl.when(x == 0)
+        def _():
+            o_sm[0:1, :] = everything[0:1]
+
+        @pl.when(x == 1)
+        def _():
+            o_sm[0:1, :] = everything[1:2]
+
+        o_sm[1:2, :] = jnp.broadcast_to(
+            jnp.sqrt(total(everything[2:3]) * (1.0 / (4 * R * N * D))), (1, D)
+        )
 
         serve_all_sent()
         waited = {id(n2_y), id(n2_core), id(y_proj)}
@@ -850,6 +888,8 @@
             dict(R=R, H=R // 2, D=D, C=C, FF=FF, NH=NH, N=N)
         )
         vmem = pl.BlockSpec(memory_space=pltpu.VMEM)
+        smem = pl.BlockSpec(memory_space=pltpu.SMEM)
+        anywhere = pl.BlockSpec(memory_space=pl.ANY)
         block_io, grads, small = pl.pallas_call(
             body,
             out_shape=(
@@ -857,25 +897,57 @@
                 jax.ShapeDtypeStruct((grad_rows, D), BF),
                 jax.ShapeDtypeStruct((8, D), F32),
             ),
-            in_specs=[pl.BlockSpec(memory_space=pltpu.SMEM)] + [vmem] * 7,
+            in_specs=[smem, vmem] + [anywhere] * 6,
             out_specs=(vmem,) * 3,
             scratch_shapes=scratch,
             compiler_params=pltpu.CompilerParams(
                 collective_id=0, has_side_effects=True, vmem_limit_bytes=62 << 20
             ),
-        )(lengths, norm_gains, stream_in, cotangent, w_qkv, w_attn_out, w_up, w_down)
-        gain = jnp.where(lax.axis_index("blk") == 0, small[0:1], small[1:2])
-        entries = 4 * R * N * D
-        stream_rms = jnp.sqrt(jnp.sum(small[2]) / entries)
-        return (
-            block_io,
-            gain,
-            grads[QKV:].T.astype(F32),
-            grads[OUT:QKV, :C].astype(F32),
-            grads[UP:OUT].astype(F32),
-            grads[DOWN:UP, :C].astype(F32),
-            stream_rms,
-        )
+        )(lengths, norm_gains, stream_in, cotangent, w_qkv.T, w_attn_out, w_up, w_down)
+
+        def spread(io_in, down_in, up_in, out_in, qkv_in, small_in, io, gain, qkv, out, up, down, rms):
+            io[...] = io_in[...]
+            down[...] = down_in[:, :C].astype(F32)
+            up[...] = up_in[...].astype(F32)
+            out[...] = out_in[:, :C].astype(F32)
+            qkv[...] = qkv_in[...].astype(F32)
+            gain[...] = small_in[0:1, :]
+            rms[0, 0] = jnp.max(small_in[1:2, :])
+
+        steps = 6
+        QW, AW = grad_rows - QKV, QKV - OUT
+        sizes = (FF // steps, D // steps, AW // steps, QW // steps)
+        firsts = (DOWN, UP, OUT, QKV)
+        piece_specs = [
+            pl.BlockSpec((n, D), lambda i, o=first // n: (o + i, 0))
+            for n, first in zip(sizes, firsts, strict=True)
+        ]
+        io_spec = pl.BlockSpec((1, R // 4, C), lambda i: (0, jnp.minimum(i, 3), 0))
+        whole = lambda i: (0, 0)
+        block_io, gain, grad_qkv, grad_out, grad_up, grad_down, rms = pl.pallas_call(
+            spread,
+            grid=(steps,),
+            out_shape=(
+                jax.ShapeDtypeStruct((1, R, C), BF),
+                jax.ShapeDtypeStruct((1, D), F32),
+                jax.ShapeDtypeStruct((QW, D), F32),
+                jax.ShapeDtypeStruct((AW, C), F32),
+                jax.ShapeDtypeStruct((D, FF), F32),
+                jax.ShapeDtypeStruct((FF, C), F32),
+                jax.ShapeDtypeStruct((1, 1), F32),
+            ),
+            in_specs=[io_spec, *piece_specs, pl.BlockSpec((8, D), whole)],
+            out_specs=(
+                io_spec,
+                pl.BlockSpec((1, D), whole),
+                pl.BlockSpec((sizes[3], D), lambda i: (i, 0)),
+                pl.BlockSpec((sizes[2], C), lambda i: (i, 0)),
+                pl.BlockSpec((sizes[1], FF), lambda i: (i, 0)),
+                pl.BlockSpec((sizes[0], C), lambda i: (i, 0)),
+                smem,
+            ),
+        )(block_io, grads, grads, grads, grads, small)
+        return (block_io, gain, grad_qkv.T, grad_out, grad_up, grad_down, rms.reshape(()))
 
     return run
 

time: 249 us -> 218 us (0.88)
  Pallas kernels: 234 us -> 216 us
  other arithmetic: 9.58 us -> 0 us
  local copies, waits for them, and re-layouts: 3.11 us -> 0 us
    pallas_call x1, Pallas kernels: 234 us -> 209 us  [run(): pl.pallas_call(body, out_shape=(jax.ShapeDtypeStruct((1, R, C), BF), jax....]
    convert_element_type x4 -> x0, other arithmetic: 7.47 us -> none  [the longest x1 2.5 us: run(): grads[QKV:].T.astype(F32)]
    pallas_call x0 -> x1, Pallas kernels: none -> 7.13 us  [run(): pl.pallas_call(spread, grid=(steps,), out_shape=(jax.ShapeDtypeStruct((1,...]
    unnamed x6 -> x0, local copies, waits for them, and re-layouts: 3.11 us -> none
where the time goes in v2:
time: 218 us; the launch traced here: 217 us
  Pallas kernels  216 us (99%)
    pallas_call x1, Pallas kernels, run(): pl.pallas_call(body, out_shape=(jax.ShapeDtypeStruct((1, R, C), BF), jax....  209 us
    pallas_call x1, Pallas kernels, run(): pl.pallas_call(spread, grid=(steps,), out_shape=(jax.ShapeDtypeStruct((1,...  7.13 us

profile of v2, /device:TPU:0, one launch (start us, length us, event | category | flops | bytes accessed | tf_op | source)
XLA Modules:
  0.0 216.5 jit_solution(9688285669351955016)
XLA Ops:
  0.6 208.8 %shard_map.135 = (bf16[1,512,767]{2,1,0:T(8,128)(2,1)}, bf16[2304,768]{1,0:T(8,128)(2,1)}, f32[8,768]{1,0:T(8,128)}) custom-call(s32[4]{0:T(128)} %lens.1, f32[1,768]{1,0:T(1,128)} %gains.1, bf16[512,767]{1,0:T(8,128)(2,1)} %stream.1, bf16[512,767]{1,0:T(8,128)(2,1)} %cot_in.1, bf16[576,768]{1,0:T(8,128)(2,1)} %bitcast.3, bf16[192,767]{1,0:T(8,128)(2,1)} %w_ao.1, ...), custom_call_target="tpu_custom_call" | custom-call | tf_op jit(solution)/shard_map/pallas_call | solution.py:893
  209.4 7.1 %shard_map.136 = (bf16[1,512,767]{2,1,0:T(8,128)(2,1)}, f32[1,768]{1,0:T(1,128)}, f32[576,768]{1,0:T(8,128)}, f32[192,767]{1,0:T(8,128)}, f32[768,768]{1,0:T(8,1...) custom-call(bf16[1,512,767]{2,1,0:T(8,128)(2,1)} %get-tuple-element.17.io_in, ...), custom_call_target="tpu_custom_call" | custom-call | tf_op jit(solution)/shard_map/pallas_call | solution.py:927

commit v3 on v2

--- a/solution.py
+++ b/solution.py
@@ -13,7 +13,10 @@
 BF = jnp.bfloat16
 F32 = jnp.float32
 MESH = pl.DeviceIdType.MESH
-PIECE = 96
+SUB = 48
+LAG = 2
+BEFORE = (1, 2, 1, 1, 2)
+UNIT, BLOCK = 0, 1
 ROOT = 0.7978845608028654
 
 
@@ -41,7 +44,8 @@
     R, H, D, C, FF, NH, N = (sizes[k] for k in ("R", "H", "D", "C", "FF", "NH", "N"))
     QW = NH * 3 * HS
     AW = NH * HS
-    PIECES = (2 * D + AW + QW) // PIECE
+    GRADS = 2 * D + AW + QW
+    GROUPS = GRADS // (3 * SUB)
     DOWN, UP, OUT, QKV = 0, FF, FF + D, FF + D + AW
     half_n = N // 2
 
@@ -57,7 +61,7 @@
     scratch("wao_in", (AW, C), BF)
     scratch("wup", (D, FF), BF)
     scratch("wdn_in", (FF, C), BF)
-    scratch("sp", (R, D), BF)
+    scratch("normed", (4 * R, D), BF)
     scratch("wao", (AW, D), BF)
     scratch("wdn", (FF, D), BF)
     scratch("n1", (4 * R, D), BF)
@@ -65,7 +69,7 @@
     scratch("k", (NH, 4 * R, HS), BF)
     scratch("v", (NH, 4 * R, HS), BF)
     scratch("e", (10 * NH, H, R), BF)
-    scratch("il", (NH, 4 * H, 1), F32)
+    scratch("il", (4 * H, 128), F32)
     scratch("att", (4 * H, AW), BF)
     scratch("proj", (4, H, D), BF)
     scratch("rsc", (2, H, D), BF)
@@ -89,17 +93,14 @@
     scratch("rscf", (2, R, D), BF)
     scratch("rsyf", (R, D), BF)
     scratch("rsxf", (R, D), BF)
-    scratch("gsrc", (PIECES * PIECE, D), BF)
-    scratch("gb", (PIECES * PIECE // 2, D), BF)
-    scratch("gc", (PIECES * PIECE // 2, D), BF)
+    scratch("gsrc", (GRADS, D), BF)
+    scratch("gb", ((GROUPS + -(-GROUPS // 4)) * SUB, D), BF)
+    scratch("gc", ((GROUPS + -(-GROUPS // 2)) * SUB, D), BF)
     scratch("sm", (5, 8, D), F32)
     scratch("smr", (3, 8, D), F32)
     scratch("smz", (N, 8, D), F32)
     n_vmem = len(names)
-    S_SRC, S_PART, S_OUT = 0, PIECES, 2 * PIECES
-    R_A, R_B, R_C, R_RES = 0, PIECES, 2 * PIECES, 3 * PIECES
-    FIRST = 4 * PIECES
-    N_SEM = FIRST + 64 + N
+    N_SEM = 10 * GROUPS + 64 + N
     scratch_shapes = list(names.values()) + [
         pltpu.SemaphoreType.DMA((N_SEM,)),
         pltpu.SemaphoreType.DMA((N_SEM,)),
@@ -123,7 +124,7 @@
         core, ydev, xdev = (x, d, t1), (x, d, t2), (1 - x, d, t)
         xh, oh = x * H, (1 - x) * H
 
-        counter = [FIRST]
+        counter = [10 * GROUPS]
         pending = []
 
         def link(src, dst, dev, s_idx=None, r_idx=None):
@@ -190,28 +191,17 @@
 
         m.gbuf[x] = jnp.broadcast_to(gains[...], (8, D))
         gain_copy = send(m.gbuf.at[x], m.gbuf.at[x], xdev)
-        m.sp[:, D - 128 :] = jnp.zeros((R, 128), BF)
         loads[0].wait()
-        m.sp[:, :C] = m.stream[...]
+        own_rows = rows(t * R, R, R)
+        m.n1[own_rows, D - 128 :] = jnp.zeros((R, 128), BF)
+        m.n1[own_rows, :C] = m.stream[...]
         here = rows(t * H, H, H)
-        gain_copy.wait_recv()
-
-        def norm_one(start, count):
-            def step(i, _):
-                r0 = start + i * 64
-                full, r = full_of(m.sp[rows(r0, 64, 64), :].astype(F32))
-                m.n1[rows(t * R + r0, 64, 64), :] = (full * r * m.gbuf[0, :1, :]).astype(BF)
-                return 0
-
-            lax.fori_loop(0, count // 64, step, 0)
 
         half = H // 4
         y_copies = []
         for k in range(4):
-            norm_one(xh + k * half, half)
             part = m.n1.at[rows(t * R + xh + k * half, half, half)]
             y_copies.append(send(part, part, ydev))
-        norm_one(oh, H)
         part = m.n1.at[rows(t * R, R, R)]
         own_copy = send(part, part, core)
         loads[2].wait()
@@ -221,7 +211,14 @@
         cot_core = send(part, part, core)
 
         def qkv_rows(start):
-            mixed = dot_nt(m.n1[rows(start, H, H), :], m.wqkv[...])
+            def step(i, _):
+                some = rows(start + i * 64, 64, 64)
+                full, r = full_of(m.n1[some, :].astype(F32))
+                m.normed[some, :] = (full * r * m.gbuf[0, :1, :]).astype(BF)
+                return 0
+
+            lax.fori_loop(0, H // 64, step, 0)
+            mixed = dot_nt(m.normed[rows(start, H, H), :], m.wqkv[...])
             at = rows(start, H, H)
             for h in range(NH):
                 for p, ref in enumerate((m.q, m.k, m.v)):
@@ -234,6 +231,7 @@
             lax.fori_loop(0, 2, lambda i, _: (qkv_rows(block * R + i * H), 0)[1], 0)
 
         loads[1].wait()
+        gain_copy.wait_recv()
         qkv_block(t)
         own_copy.wait_recv()
         qkv_block(t1)
@@ -277,7 +275,7 @@
         def unit(b, kb):
             return lax.div(b * (b + 1), 2) + kb
 
-        def attend(b):
+        def attend(b, between):
             mine = rows(b * R + xh, H, H)
             heads = [m.q[h, mine, :] for h in range(NH)]
 
@@ -294,15 +292,19 @@
 
             def peak(kb, best):
                 bias = bias_of(b, kb)
-                return tuple(top(scores(h, kb) + bias, best[h]) for h in range(NH))
+                low = jnp.full((H, 128), -jnp.inf, F32)
+                return tuple(
+                    jnp.maximum(best[h], top(scores(h, kb), low) + bias) for h in range(NH)
+                )
 
             low = jnp.full((H, 128), MASKED, F32)
             best = tuple(top(masked(scores(h, b)), low) for h in range(NH))
             best = lax.fori_loop(0, b, peak, best)
             best = [jnp.max(v, axis=1, keepdims=True) for v in best]
-
-            def weigh(h, kb, s, sums, acc):
-                e = jnp.exp(s - best[h])
+            between()
+
+            def weigh(h, kb, s, off, sums, acc):
+                e = jnp.exp(s - off)
                 for g in lane_groups(e):
                     sums = sums + g
                 e = e.astype(BF)
@@ -311,15 +313,17 @@
 
             def add(kb, carry):
                 bias = bias_of(b, kb)
-                return tuple(weigh(h, kb, scores(h, kb) + bias, *carry[h]) for h in range(NH))
+                return tuple(
+                    weigh(h, kb, scores(h, kb), best[h] - bias, *carry[h]) for h in range(NH)
+                )
 
             zero = (jnp.zeros((H, 128), F32), jnp.zeros((H, HS), F32))
-            carry = tuple(weigh(h, b, masked(scores(h, b)), *zero) for h in range(NH))
+            carry = tuple(weigh(h, b, masked(scores(h, b)), best[h], *zero) for h in range(NH))
             carry = lax.fori_loop(0, b, add, carry)
             at = rows(b * H, H, H)
             for h in range(NH):
                 inverse = 1.0 / total(carry[h][0])
-                m.il[h, at, :] = inverse
+                m.il[at, h : h + 1] = inverse
                 m.att[at, h * HS : (h + 1) * HS] = (carry[h][1] * inverse).astype(BF)
             return dot_nn(m.att[at, :], m.wao[...]).astype(BF)
 
@@ -344,17 +348,19 @@
         def attend_step(i, _):
             a, e = lax.div(i, 2), 1 - lax.rem(i, 2)
             g = (1 - y) * (1 - a) + y * a
-            m.proj[i] = attend(2 * g + e)
+
+            def between():
+                @pl.when(i == 2 - c)
+                def _():
+                    proj_copy(c).wait_recv()
+                    add_rows(m.ysnd, (m.proj.at[1 - c], m.rsc.at[0]), H)
+                    y_proj.start()
+
+            m.proj[i] = attend(2 * g + e, between)
 
             @pl.when(lax.rem(i, 2) == c)
             def _():
                 proj_copy(i).start()
-
-            @pl.when(i == 2)
-            def _():
-                proj_copy(c).wait_recv()
-                add_rows(m.ysnd, (m.proj.at[1 - c], m.rsc.at[0]), H)
-                y_proj.start()
 
             return 0
 
@@ -368,7 +374,7 @@
 
         def middle_step(i, squares):
             at = rows(i * 64, 64, 64)
-            mid = m.sp[rows(xh + i * 64, 64, 64), :].astype(F32)
+            mid = m.n1[rows(t * R + xh + i * 64, 64, 64), :].astype(F32)
             mid = mid + m.proj[2 + 1 - c, at, :].astype(F32)
             mid = mid + m.rsc[1, at, :].astype(F32) + m.rsy[at, :].astype(F32)
             mid = mid.astype(BF)
@@ -454,123 +460,274 @@
         inner = (x, lax.rem(d + step_in + N, N), t)
         outer = (x, lax.rem(d - step_in + N, N), t)
 
-        def piece(ref, p):
-            return ref.at[rows(p * PIECE, PIECE, 16)]
-
-        def in_copy(p):
-            return link(piece(m.gsrc, p), piece(res, p), inner, S_SRC + p, R_A + p)
-
-        def mid_copy(p):
-            to = piece(m.gb, lax.div(p, 2))
-            return link(piece(m.gsrc, p), to, inner, S_SRC + p, R_B + p)
-
-        def x_copy(p):
-            to = piece(m.gc, lax.div(p, 2))
-            return link(piece(m.gsrc, p), to, xdev, S_SRC + p, R_C + p)
-
-        def part_copy(p):
-            return link(piece(res, p), piece(res, p), inner, S_PART + p, R_RES + p)
-
-        def out_copy(p):
-            return link(piece(res, p), piece(res, p), outer, S_OUT + p, R_RES + p)
-
-        def gather_piece(out, p, ref, q):
-            def step(i, _):
-                at = rows(p * PIECE + i * 32, 32, 16)
-                other = ref[rows(q * PIECE + i * 32, 32, 16), :].astype(F32)
-                out[at, :] = (m.gsrc[at, :].astype(F32) + other).astype(BF)
+        not_end = jnp.logical_not(is_end)
+
+        def sub_rows(ref, at, count):
+            return ref.at[rows(at, count * SUB, 16)]
+
+        def group_at(g):
+            return g * (3 * SUB)
+
+        def third_at(g):
+            return group_at(g) + 2 * SUB
+
+        def sub_at(g, who):
+            return group_at(g) + who * SUB
+
+        def sem(kind, g):
+            return kind * GROUPS + g
+
+        def in_copy(g):
+            at = group_at(g)
+            return link(sub_rows(m.gsrc, at, 2), sub_rows(res, at, 2), inner, sem(0, g), sem(0, g))
+
+        def mid_copy(g):
+            src = sub_rows(m.gsrc, sub_at(g, 1 - side), 1)
+            return link(src, sub_rows(m.gb, g * SUB, 1), inner, sem(1, g), sem(1, g))
+
+        def blk_copy(g):
+            src = sub_rows(m.gsrc, sub_at(g, side), 1)
+            return link(src, sub_rows(m.gc, g * SUB, 1), xdev, sem(2, g), sem(2, g))
+
+        def res_link(g, who, dev, kind):
+            at = sub_rows(res, sub_at(g, who), 1)
+            return link(at, at, dev, sem(kind, g), sem(3, g) + GROUPS * who)
+
+        def own_part(g):
+            return res_link(g, side, inner, 3)
+
+        def own_out(g):
+            return res_link(g, side, outer, 4)
+
+        def other_part(g):
+            return res_link(g, 1 - side, inner, 3)
+
+        def other_out(g):
+            return res_link(g, 1 - side, outer, 5)
+
+        def c_link(dst, dev, kind):
+            def make(g):
+                src = sub_rows(m.gsrc, third_at(g), 1)
+                return link(src, dst(g), dev, sem(6, g), sem(kind, g))
+
+            return make
+
+        def c_res(dev, kind):
+            def make(g):
+                at = sub_rows(res, third_at(g), 1)
+                return link(at, at, dev, sem(kind, g), sem(8, g))
+
+            return make
+
+        c_blk = c_link(lambda g: sub_rows(m.gc, (GROUPS + lax.div(g, 2)) * SUB, 1), xdev, 5)
+        c_in = c_link(lambda g: sub_rows(res, third_at(g), 1), inner, 6)
+        c_mid = c_link(lambda g: sub_rows(m.gb, (GROUPS + lax.div(g, 4)) * SUB, 1), inner, 7)
+        c_part, c_out, c_back = c_res(inner, 7), c_res(outer, 8), c_res(xdev, 9)
+
+        def add(out, at, other, count):
+            for k in range(count):
+                here_rows = rows(at + k * SUB, SUB, 16)
+                there = other[k * SUB : (k + 1) * SUB, :].astype(F32)
+                out[here_rows, :] = (m.gsrc[here_rows, :].astype(F32) + there).astype(BF)
+
+        def valid(g):
+            return (g >= 0) & (g < GROUPS)
+
+        def mine(g):
+            return x == lax.rem(g + 2 * GROUPS, 2)
+
+        def late_owns(g):
+            return side == lax.rem(lax.div(g + 4 * GROUPS, 2), 2)
+
+        def serve(s):
+            g1, g2, g3, g4, g5, g6 = (s - i * LAG for i in range(6))
+
+            @pl.when(valid(g1) & jnp.logical_not(mine(g1)))
+            def _():
+                c_blk(g1).start()
+
+            @pl.when(jnp.logical_not(is_mid))
+            def _():
+                @pl.when(valid(g1))
+                def _():
+                    if N > 4:
+
+                        @pl.when(not_end)
+                        def _():
+                            in_copy(g1).wait_recv()
+                            add(m.gsrc, group_at(g1), sub_rows(res, group_at(g1), 2), 2)
+
+                    in_copy(g1).start()
+
+                @pl.when(valid(g2) & mine(g2))
+                def _():
+                    c_blk(g2).wait_recv()
+                    add(m.gsrc, third_at(g2), sub_rows(m.gc, (GROUPS + lax.div(g2, 2)) * SUB, 1), 1)
+                    if N > 4:
+
+                        @pl.when(not_end)
+                        def _():
+                            c_in(g2).wait_recv()
+                            add(m.gsrc, third_at(g2), sub_rows(res, third_at(g2), 1), 1)
+
+                    c_in(g2).start()
+
+                @pl.when(valid(g6))
+                def _():
+                    if N > 4:
+
+                        @pl.when(not_end)
+                        def _():
+                            own_out(g6).wait_recv()
+                            own_out(g6).start()
+                            other_out(g6).wait_recv()
+                            other_out(g6).start()
+
+                    @pl.when(mine(g6))
+                    def _():
+                        c_part(g6).wait_recv()
+                        c_back(g6).start()
+                        if N > 4:
+
+                            @pl.when(not_end)
+                            def _():
+                                c_out(g6).start()
+
+            @pl.when(is_mid)
+            def _():
+                @pl.when(valid(g2))
+                def _():
+                    if N > 2:
+
+                        @pl.when(not_end)
+                        def _():
+                            in_copy(g2).wait_recv()
+                            add(m.gsrc, group_at(g2), sub_rows(res, group_at(g2), 2), 2)
+
+                    mid_copy(g2).start()
+
+                    @pl.when(mine(g2))
+                    def _():
+                        c_blk(g2).wait_recv()
+                        add(m.gsrc, third_at(g2), sub_rows(m.gc, (GROUPS + lax.div(g2, 2)) * SUB, 1), 1)
+
+                @pl.when(valid(g3))
+                def _():
+                    mid_copy(g3).wait_recv()
+                    add(m.gsrc, sub_at(g3, side), sub_rows(m.gb, g3 * SUB, 1), 1)
+                    blk_copy(g3).start()
+
+                    @pl.when(mine(g3))
+                    def _():
+                        if N > 2:
+
+                            @pl.when(not_end)
+                            def _():
+                                c_in(g3).wait_recv()
+                                add(m.gsrc, third_at(g3), sub_rows(res, third_at(g3), 1), 1)
+
+                        @pl.when(jnp.logical_not(late_owns(g3)))
+                        def _():
+                            c_mid(g3).start()
+
+                @pl.when(valid(g4))
+                def _():
+                    blk_copy(g4).wait_recv()
+                    add(res, sub_at(g4, side), sub_rows(m.gc, g4 * SUB, 1), 1)
+                    own_part(g4).start()
+                    if N > 2:
+
+                        @pl.when(not_end)
+                        def _():
+                            own_out(g4).start()
+
+                    @pl.when(mine(g4) & late_owns(g4))
+                    def _():
+                        c_mid(g4).wait_recv()
+                        add(res, third_at(g4), sub_rows(m.gb, (GROUPS + lax.div(g4, 4)) * SUB, 1), 1)
+                        c_part(g4).start()
+                        c_back(g4).start()
+                        if N > 2:
+
+                            @pl.when(not_end)
+                            def _():
+                                c_out(g4).start()
+
+                @pl.when(valid(g5))
+                def _():
+                    other_part(g5).wait_recv()
+                    if N > 2:
+
+                        @pl.when(not_end)
+                        def _():
+                            other_out(g5).start()
+
+                    @pl.when(mine(g5) & jnp.logical_not(late_owns(g5)))
+                    def _():
+                        c_part(g5).wait_recv()
+                        c_back(g5).start()
+                        if N > 2:
+
+                            @pl.when(not_end)
+                            def _():
+                                c_out(g5).start()
+
+        def serve_range(begin, end):
+            lax.fori_loop(begin, end, lambda s, _: (serve(s), 0)[1], 0)
+
+        def serve_all_sent():
+            def step(g, _):
+                @pl.when(jnp.logical_not(is_mid))
+                def _():
+                    @pl.when(is_end)
+                    def _():
+                        own_part(g).wait_recv()
+                        other_part(g).wait_recv()
+
+                    in_copy(g).wait_send()
+
+                @pl.when(is_mid)
+                def _():
+                    mid_copy(g).wait_send()
+                    blk_copy(g).wait_send()
+                    own_part(g).wait_send()
+
+                @pl.when(not_end)
+                def _():
+                    own_out(g).wait_send()
+                    other_out(g).wait_send()
+
+                ended = mine(g) & is_mid & late_owns(g)
+
+                @pl.when(jnp.logical_not(ended))
+                def _():
+                    c_in(g).wait_send()
+
+                @pl.when(ended)
+                def _():
+                    c_part(g).wait_send()
+
+                @pl.when(mine(g))
+                def _():
+                    c_back(g).wait_send()
+
+                @pl.when(mine(g) & not_end)
+                def _():
+                    c_out(g).wait_send()
+
+                @pl.when(jnp.logical_not(mine(g)))
+                def _():
+                    c_part(g).wait_recv()
+
                 return 0
 
-            lax.fori_loop(0, PIECE // 32, step, 0)
-
-        def valid(p):
-            return (p >= 0) & (p < PIECES)
-
-        def owns(p):
-            return is_mid & (side == lax.rem(p + 2 * PIECES, 2))
-
-        def serve(s):
-            @pl.when(valid(s) & jnp.logical_not(is_mid))
-            def _():
-                if N > 4:
-
-                    @pl.when(jnp.logical_not(is_end))
-                    def _():
-                        in_copy(s).wait_recv()
-                        gather_piece(m.gsrc, s, res, s)
-
-                in_copy(s).start()
-
-            p2 = s - 2
-
-            @pl.when(valid(p2) & is_mid)
-            def _():
-                @pl.when(jnp.logical_not(is_end))
-                def _():
-                    in_copy(p2).wait_recv()
-                    gather_piece(m.gsrc, p2, res, p2)
-
-                @pl.when(jnp.logical_not(owns(p2)))
-                def _():
-                    mid_copy(p2).start()
-
-            p3 = s - 4
-
-            @pl.when(valid(p3) & owns(p3))
-            def _():
-                mid_copy(p3).wait_recv()
-                gather_piece(m.gsrc, p3, m.gb, lax.div(p3, 2))
-                x_copy(p3).start()
-
-            p4 = s - 6
-
-            @pl.when(valid(p4) & owns(p4))
-            def _():
-                x_copy(p4).wait_recv()
-                gather_piece(res, p4, m.gc, lax.div(p4, 2))
-                part_copy(p4).start()
-
-                @pl.when(jnp.logical_not(is_end))
-                def _():
-                    out_copy(p4).start()
-
-            p5 = s - 8
-
-            @pl.when(valid(p5) & is_mid & jnp.logical_not(owns(p5)))
-            def _():
-                part_copy(p5).wait_recv()
-
-                @pl.when(jnp.logical_not(is_end))
-                def _():
-                    out_copy(p5).start()
-
-            if N > 4:
-                p6 = s - 10
-
-                @pl.when(valid(p6) & jnp.logical_not(is_mid) & jnp.logical_not(is_end))
-                def _():
-                    part_copy(p6).wait_recv()
-                    out_copy(p6).start()
-
-        def serve_all_sent():
-            def step(p, _):
-                @pl.when(is_end & jnp.logical_not(is_mid))
-                def _():
-                    part_copy(p).wait_recv()
-
-                in_copy(p).wait_send()
-
-                @pl.when(owns(p))
-                def _():
-                    part_copy(p).wait_send()
-
-                @pl.when(jnp.logical_not(is_end))
-                def _():
-                    out_copy(p).wait_send()
-
-                return 0
-
-            lax.fori_loop(0, PIECES, step, 0)
+            lax.fori_loop(0, GROUPS, step, 0)
+
+        tail = [0]
+
+        def serve_next(count):
+            serve_range(tail[0], tail[0] + count)
+            tail[0] += count
 
         def down_step(f, _):
             at = pl.ds(pl.multiple_of(f * 256, 256), 256)
@@ -582,8 +739,25 @@
             m.gsrc[rows(UP + f * 256, 256, 16), :] = dot_tn(m.n2[:, at], m.gh[...]).astype(BF)
             return 0
 
-        lax.fori_loop(0, FF // 256, down_step, 0)
-        serve(0)
+        down_step(0, 0)
+        serve_next(BEFORE[0])
+        down_step(1, 0)
+        down_step(2, 0)
+        serve_next(BEFORE[1])
+        lax.fori_loop(0, D // 256, up_step, 0)
+        serve_next(BEFORE[2])
+
+        def mlp_step(i, _):
+            a, e = lax.div(i, 2), lax.rem(i, 2)
+            s = 2 * (y + a - 2 * y * a) + (c + e - 2 * c * e)
+            m.proj[i] = dot_nn(m.act[rows(s * H, H, H), :], m.wdn[...]).astype(BF)
+            return 0
+
+        proj_copy(c).wait_send()
+        proj_copy(2 + c).wait_send()
+        lax.fori_loop(0, 4, mlp_step, 0)
+        mp_copies = [send(m.proj.at[2 * j + 1], m.rsc.at[j], core) for j in range(2)]
+        serve_next(BEFORE[3])
 
         gp_copies[0].wait_recv()
         gp_y.wait_recv()
@@ -608,20 +782,7 @@
         def _():
             gm_x.start()
 
-        lax.fori_loop(0, D // 256, up_step, 0)
-        serve(1)
-
-        def mlp_step(i, _):
-            a, e = lax.div(i, 2), lax.rem(i, 2)
-            s = 2 * (y + a - 2 * y * a) + (c + e - 2 * c * e)
-            m.proj[i] = dot_nn(m.act[rows(s * H, H, H), :], m.wdn[...]).astype(BF)
-            return 0
-
-        proj_copy(c).wait_send()
-        proj_copy(2 + c).wait_send()
-        lax.fori_loop(0, 4, mlp_step, 0)
-        mp_copies = [send(m.proj.at[2 * j + 1], m.rsc.at[j], core) for j in range(2)]
-        serve(2)
+        serve_next(BEFORE[4])
         gm_y.wait_recv()
         part = m.gm.at[rows(t2 * H, H, H)]
         gm_fwd = send(part, part, core)
@@ -673,6 +834,10 @@
             lax.fori_loop(0, 4, step, 0)
 
         far_step = 3 - (2 * (1 - y) + c)
+        BACK = sum(BEFORE)
+
+        def back_served(i, units):
+            return BACK + UNIT * (4 * i - lax.div(i * (i - 1), 2) + units) + BLOCK * i
 
         def back_block(i, _):
             b = 3 - i
@@ -682,7 +847,7 @@
             outs, offs, out_ts, q_ts = [], [], [], []
             for h in range(NH):
                 cols = slice(h * HS, (h + 1) * HS)
-                inverse = m.il[h, at, :]
+                inverse = m.il[at, h : h + 1]
                 out = grad_att[:, cols].astype(BF).astype(F32)
                 delta = total(out * m.att[at, cols].astype(F32))
                 offs.append(delta * inverse)
@@ -701,7 +866,7 @@
                     new.append(grads[h] + dot_nn(ds, m.k[h, at_k, :]))
                     m.dkt[kb, h] += dot_nn(q_ts[h], ds)
                     m.dvt[kb, h] += dot_nn(out_ts[h], e)
-                serve(3 + 4 * i - lax.div(i * (i - 1), 2) + kb)
+                serve_range(back_served(i, kb), back_served(i, kb + 1))
                 return tuple(new)
 
             grads = lax.fori_loop(0, b + 1, keys, (jnp.zeros((H, HS), F32),) * NH)
@@ -713,7 +878,7 @@
                 m.dmt[base + HS : base + 2 * HS, :] = m.dkt[b, h].astype(BF)
                 m.dmt[base + 2 * HS : base + 3 * HS, :] = m.dvt[b, h].astype(BF)
             n1_rows = rows(b * R, R, R)
-            m.gq[...] += dot_nn(m.dmt[...], m.n1[n1_rows, :])
+            m.gq[...] += dot_nn(m.dmt[...], m.normed[n1_rows, :])
             back = dot_nn(jnp.transpose(m.dmt[...]), m.wqkv[...]).astype(BF)
             j = lax.div(b, 2)
 
@@ -725,6 +890,8 @@
             def _():
                 m.gh[pair_rows(j), :] = back
                 gn_copy(j).start()
+
+            serve_range(back_served(i, b + 1), back_served(i + 1, 0))
 
             @pl.when(i == far_step + 1)
             def _():
@@ -735,8 +902,7 @@
         lax.fori_loop(0, 4, back_block, 0)
         pl.when(far_step == 3)(send_far)
         m.gsrc[QKV : QKV + QW, :] = m.gq[...].astype(BF)
-        served = 13
-
+        tail[0] = BACK + 10 * UNIT + 4 * BLOCK
         mp_copies[0].wait_recv()
         mp_y.wait_recv()
         n2_y.wait_send()
@@ -748,7 +914,7 @@
         def _():
             bo_x.start()
 
-        lax.fori_loop(served, 18, lambda s, _: (serve(s), 0)[1], 0)
+        serve_next(2)
 
         gn_copy(y).wait_recv()
 
@@ -773,22 +939,29 @@
 
             lax.fori_loop(0, chunk // 64, inside, 0)
 
-        @pl.when(x == 1)
-        def _():
-            def step(k, _):
-                near_sum(k)
+        first = tail[0]
+        tail[0] += 2
+
+        def near_step(k, _):
+            serve_range(first + lax.div(k, 2), first + lax.div(k + 1, 2))
+            near_sum(k)
+
+            @pl.when(x == 1)
+            def _():
                 xf_copy(k).start()
-                return 0
-
-            lax.fori_loop(0, 4, step, 0)
-
-        @pl.when(x == 0)
-        def _():
-            gm_x.wait_recv()
-            m.sm[0, 0:1, :] = jnp.zeros((1, D), F32)
-
-            def step(k, _):
-                near_sum(k)
+
+            return 0
+
+        lax.fori_loop(0, 4, near_step, 0)
+        m.sm[0, 0:1, :] = jnp.zeros((1, D), F32)
+        then = tail[0]
+        tail[0] += 2
+
+        def grad_in_step(k, _):
+            serve_range(then + lax.div(k, 2), then + lax.div(k + 1, 2))
+
+            @pl.when(x == 0)
+            def _():
                 xf_copy(k).wait_recv()
 
                 def inside(i, gain):
@@ -796,16 +969,21 @@
                     here_rows = rows(r0, 64, 64)
                     grad = m.act[rows(y * R + r0, 64, 64), :].astype(F32)
                     grad = grad + m.rsxf[here_rows, :].astype(F32)
-                    full, r = full_of(m.sp[here_rows, :].astype(F32))
+                    full, r = full_of(m.n1[rows(t * R + r0, 64, 64), :].astype(F32))
                     back = crms_back(grad, full, r, m.gbuf[0, :1, :])
                     m.rsyf[here_rows, :] = back.astype(BF)
                     return gain + jnp.sum(grad * full * r, axis=0, keepdims=True)
 
                 gain = lax.fori_loop(0, chunk // 64, inside, jnp.zeros((1, D), F32))
                 m.sm[0, 0:1, :] += gain
-                return 0
-
-            lax.fori_loop(0, 4, step, 0)
+
+            return 0
+
+        lax.fori_loop(0, 4, grad_in_step, 0)
+
+        @pl.when(x == 0)
+        def _():
+            gm_x.wait_recv()
 
             def out_step(i, _):
                 at = rows(i * 64, 64, 64)
@@ -826,12 +1004,13 @@
 
         for j, peer in enumerate((core, ydev, xdev)):
             copy = send(m.sm.at[j], m.smr.at[j], peer)
+            serve_next(1)
             copy.wait_recv()
             m.sm[j + 1] = m.sm[j] + m.smr[j]
         z_copies = []
         for j in range(1, N):
             z_copies.append(send(m.sm.at[3], m.smz.at[j], (x, lax.rem(d + j, N), t)))
-        lax.fori_loop(18, PIECES + 12, lambda s, _: (serve(s), 0)[1], 0)
+        serve_range(tail[0], GROUPS + 5 * LAG)
         everything = m.sm[3]
         for j in range(1, N):
             z_copies[j - 1].wait_recv()
@@ -872,7 +1051,7 @@
 
         assert counter[0] <= N_SEM
 
-    return body, scratch_shapes, PIECES * PIECE, (DOWN, UP, OUT, QKV)
+    return body, scratch_shapes, GRADS, (DOWN, UP, OUT, QKV)
 
 
 def per_device(mesh):
@@ -901,7 +1080,7 @@
             out_specs=(vmem,) * 3,
             scratch_shapes=scratch,
             compiler_params=pltpu.CompilerParams(
-                collective_id=0, has_side_effects=True, vmem_limit_bytes=62 << 20
+                collective_id=0, has_side_effects=True, vmem_limit_bytes=63 << 20
             ),
         )(lengths, norm_gains, stream_in, cotangent, w_qkv.T, w_attn_out, w_up, w_down)
 

time: 218 us -> 190 us (0.87)
  Pallas kernels: 216 us -> 187 us
    pallas_call x1, Pallas kernels: 209 us -> 179 us  [run(): pl.pallas_call(body, out_shape=(jax.ShapeDtypeStruct((1, R, C), BF), jax....]
where the time goes in v3:
time: 190 us; the launch traced here: 187 us
  Pallas kernels  187 us (98%)
    pallas_call x1, Pallas kernels, run(): pl.pallas_call(body, out_shape=(jax.ShapeDtypeStruct((1, R, C), BF), jax....  179 us
    pallas_call x1, Pallas kernels, run(): pl.pallas_call(spread, grid=(steps,), out_shape=(jax.ShapeDtypeStruct((1,...  7.13 us

profile of v3, /device:TPU:0, one launch (start us, length us, event | category | flops | bytes accessed | tf_op | source)
XLA Modules:
  0.0 187.4 jit_solution(10441120641284787107)
XLA Ops:
  0.6 179.5 %shard_map.135 = (bf16[1,512,767]{2,1,0:T(8,128)(2,1)}, bf16[2304,768]{1,0:T(8,128)(2,1)}, f32[8,768]{1,0:T(8,128)}) custom-call(s32[4]{0:T(128)} %lens.1, f32[1,768]{1,0:T(1,128)} %gains.1, bf16[512,767]{1,0:T(8,128)(2,1)} %stream.1, bf16[512,767]{1,0:T(8,128)(2,1)} %cot_in.1, bf16[576,768]{1,0:T(8,128)(2,1)} %bitcast.3, bf16[192,767]{1,0:T(8,128)(2,1)} %w_ao.1, ...), custom_call_target="tpu_custom_call" | custom-call | tf_op jit(solution)/shard_map/pallas_call | solution.py:1072
  180.1 7.1 %shard_map.136 = (bf16[1,512,767]{2,1,0:T(8,128)(2,1)}, f32[1,768]{1,0:T(1,128)}, f32[576,768]{1,0:T(8,128)}, f32[192,767]{1,0:T(8,128)}, f32[768,768]{1,0:T(8,1...) custom-call(bf16[1,512,767]{2,1,0:T(8,128)(2,1)} %get-tuple-element.17.io_in, ...), custom_call_target="tpu_custom_call" | custom-call | tf_op jit(solution)/shard_map/pallas_call | solution.py:1106

commit v4 on v3

--- a/solution.py
+++ b/solution.py
@@ -15,8 +15,8 @@
 MESH = pl.DeviceIdType.MESH
 SUB = 48
 LAG = 2
-BEFORE = (1, 2, 1, 1, 2)
-UNIT, BLOCK = 0, 1
+BEFORE = (1, 2, 1, 1, 1)
+WITHIN = 6
 ROOT = 0.7978845608028654
 
 
@@ -87,6 +87,7 @@
     scratch("gm", (4 * H, D), BF)
     scratch("gother", (H, D), BF)
     scratch("dmt", (QW, R), BF)
+    scratch("dqt", (4, AW, H), BF)
     scratch("dkt", (4, NH, HS, R), F32)
     scratch("dvt", (4, NH, HS, R), F32)
     scratch("gq", (QW, D), F32)
@@ -94,6 +95,7 @@
     scratch("rsyf", (R, D), BF)
     scratch("rsxf", (R, D), BF)
     scratch("gsrc", (GRADS, D), BF)
+    scratch("res", (GRADS, D), BF)
     scratch("gb", ((GROUPS + -(-GROUPS // 4)) * SUB, D), BF)
     scratch("gc", ((GROUPS + -(-GROUPS // 2)) * SUB, D), BF)
     scratch("sm", (5, 8, D), F32)
@@ -105,14 +107,15 @@
         pltpu.SemaphoreType.DMA((N_SEM,)),
         pltpu.SemaphoreType.DMA((N_SEM,)),
         pltpu.SemaphoreType.DMA((6,)),
+        pltpu.SemaphoreType.DMA((GROUPS,)),
     ]
 
     def body(
         lens, gains, stream, cot_in, w_qkv, w_ao, w_up, w_dn, o_io, o_gr, o_sm, *refs
     ):
         m = SimpleNamespace(**dict(zip(names, refs[:n_vmem], strict=True)))
-        ssem, rsem, lsem = refs[n_vmem:]
-        res = o_gr
+        ssem, rsem, lsem, osem = refs[n_vmem:]
+        res = m.res
         x = lax.axis_index("blk")
         d = lax.axis_index("dp")
         t = lax.axis_index("tensor")
@@ -675,7 +678,11 @@
         def serve_range(begin, end):
             lax.fori_loop(begin, end, lambda s, _: (serve(s), 0)[1], 0)
 
-        def serve_all_sent():
+        def leave(g):
+            at = rows(group_at(g), 3 * SUB, 16)
+            return pltpu.make_async_copy(res.at[at], o_gr.at[at], osem.at[g])
+
+        def settle(begin, end):
             def step(g, _):
                 @pl.when(jnp.logical_not(is_mid))
                 def _():
@@ -719,9 +726,10 @@
                 def _():
                     c_part(g).wait_recv()
 
+                leave(g).start()
                 return 0
 
-            lax.fori_loop(0, GROUPS, step, 0)
+            lax.fori_loop(begin, end, step, 0)
 
         tail = [0]
 
@@ -783,17 +791,22 @@
             gm_x.start()
 
         serve_next(BEFORE[4])
-        gm_y.wait_recv()
         part = m.gm.at[rows(t2 * H, H, H)]
-        gm_fwd = send(part, part, core)
-        mp_copies[1].wait_recv()
-        y_proj.wait_send()
-        add_rows(m.ysnd, (m.proj.at[2], m.rsc.at[1]), H)
-        mp_y = send(m.ysnd, m.rsy, ydev)
+        gm_fwd = link(part, part, core)
+        mp_y = link(m.ysnd, m.rsy, ydev)
+        pending.extend((gm_fwd, mp_y))
         gm_core.wait_recv()
-        gm_fwd.wait_recv()
-
-        m.gsrc[OUT : OUT + AW, :] = dot_tn(m.att[...], m.gm[...]).astype(BF)
+
+        def far_gradient():
+            gm_y.wait_recv()
+            gm_fwd.start()
+            mp_copies[1].wait_recv()
+            y_proj.wait_send()
+            add_rows(m.ysnd, (m.proj.at[2], m.rsc.at[1]), H)
+            mp_y.start()
+            gm_fwd.wait_recv()
+            m.gsrc[OUT : OUT + AW, :] = dot_tn(m.att[...], m.gm[...]).astype(BF)
+
         m.dkt[...] = jnp.zeros_like(m.dkt)
         m.dvt[...] = jnp.zeros_like(m.dvt)
         m.gq[...] = jnp.zeros_like(m.gq)
@@ -833,14 +846,12 @@
 
             lax.fori_loop(0, 4, step, 0)
 
-        far_step = 3 - (2 * (1 - y) + c)
         BACK = sum(BEFORE)
 
-        def back_served(i, units):
-            return BACK + UNIT * (4 * i - lax.div(i * (i - 1), 2) + units) + BLOCK * i
-
         def back_block(i, _):
-            b = 3 - i
+            g = jnp.where(i < 2, y, 1 - y)
+            b = 2 * g + 1 - lax.rem(i, 2)
+            pl.when(i == 2)(far_gradient)
             at = rows(b * H, H, H)
             mine = rows(b * R + xh, H, H)
             grad_att = dot_nt(m.gm[at, :], m.wao[...])
@@ -866,19 +877,29 @@
                     new.append(grads[h] + dot_nn(ds, m.k[h, at_k, :]))
                     m.dkt[kb, h] += dot_nn(q_ts[h], ds)
                     m.dvt[kb, h] += dot_nn(out_ts[h], e)
-                serve_range(back_served(i, kb), back_served(i, kb + 1))
+                serve_range(BACK + lax.div(WITHIN * (done + kb), 10), BACK + lax.div(WITHIN * (done + kb + 1), 10))
                 return tuple(new)
 
+            done = jnp.where(y == 1, 4 * i - lax.div(i * (i - 1), 2), jnp.where(i < 2, 2 * i, 4 * i - 5))
             grads = lax.fori_loop(0, b + 1, keys, (jnp.zeros((H, HS), F32),) * NH)
             for h in range(NH):
+                grad_q = jnp.transpose(grads[h] * HS**-0.5).astype(BF)
+                m.dqt[b, h * HS : (h + 1) * HS, :] = grad_q
+            pl.when((i == 3) & (c == 1))(send_far)
+            begin = jnp.where(y == 1, i, jnp.where(i == 3, 1, 0))
+            end = jnp.where(y == 1, i + 1, jnp.where(i == 3, 4, jnp.where(i == 2, 1, 0)))
+            lax.fori_loop(begin, end, block_done, 0)
+            return 0
+
+        def block_done(f, _):
+            b = 3 - f
+            for h in range(NH):
                 base = 3 * h * HS
-                grad_q = jnp.transpose(grads[h] * HS**-0.5).astype(BF)
-                m.dmt[base : base + HS, rows(xh, H, H)] = grad_q
+                m.dmt[base : base + HS, rows(xh, H, H)] = m.dqt[b, h * HS : (h + 1) * HS, :]
                 m.dmt[base : base + HS, rows(oh, H, H)] = jnp.zeros((HS, H), BF)
                 m.dmt[base + HS : base + 2 * HS, :] = m.dkt[b, h].astype(BF)
                 m.dmt[base + 2 * HS : base + 3 * HS, :] = m.dvt[b, h].astype(BF)
-            n1_rows = rows(b * R, R, R)
-            m.gq[...] += dot_nn(m.dmt[...], m.normed[n1_rows, :])
+            m.gq[...] += dot_nn(m.dmt[...], m.normed[rows(b * R, R, R), :])
             back = dot_nn(jnp.transpose(m.dmt[...]), m.wqkv[...]).astype(BF)
             j = lax.div(b, 2)
 
@@ -891,18 +912,13 @@
                 m.gh[pair_rows(j), :] = back
                 gn_copy(j).start()
 
-            serve_range(back_served(i, b + 1), back_served(i + 1, 0))
-
-            @pl.when(i == far_step + 1)
-            def _():
-                send_far()
-
+            pl.when((y == 0) & (c == 0) & (f == 2))(send_far)
             return 0
 
         lax.fori_loop(0, 4, back_block, 0)
-        pl.when(far_step == 3)(send_far)
+        pl.when((y == 1) & (c == 0))(send_far)
         m.gsrc[QKV : QKV + QW, :] = m.gq[...].astype(BF)
-        tail[0] = BACK + 10 * UNIT + 4 * BLOCK
+        tail[0] = BACK + WITHIN
         mp_copies[0].wait_recv()
         mp_y.wait_recv()
         n2_y.wait_send()
@@ -1010,6 +1026,8 @@
         z_copies = []
         for j in range(1, N):
             z_copies.append(send(m.sm.at[3], m.smz.at[j], (x, lax.rem(d + j, N), t)))
+        settled = max(0, min(tail[0] - 5 * LAG - 1, GROUPS))
+        settle(0, settled)
         serve_range(tail[0], GROUPS + 5 * LAG)
         everything = m.sm[3]
         for j in range(1, N):
@@ -1029,7 +1047,8 @@
             jnp.sqrt(total(everything[2:3]) * (1.0 / (4 * R * N * D))), (1, D)
         )
 
-        serve_all_sent()
+        settle(settled, GROUPS)
+        lax.fori_loop(0, GROUPS, lambda g, _: (leave(g).wait(), 0)[1], 0)
         waited = {id(n2_y), id(n2_core), id(y_proj)}
         for copy in pending:
             if id(copy) not in waited:
@@ -1077,55 +1096,78 @@
                 jax.ShapeDtypeStruct((8, D), F32),
             ),
             in_specs=[smem, vmem] + [anywhere] * 6,
-            out_specs=(vmem,) * 3,
+            out_specs=(vmem, anywhere, vmem),
             scratch_shapes=scratch,
             compiler_params=pltpu.CompilerParams(
                 collective_id=0, has_side_effects=True, vmem_limit_bytes=63 << 20
             ),
         )(lengths, norm_gains, stream_in, cotangent, w_qkv.T, w_attn_out, w_up, w_down)
 
-        def spread(io_in, down_in, up_in, out_in, qkv_in, small_in, io, gain, qkv, out, up, down, rms):
-            io[...] = io_in[...]
-            down[...] = down_in[:, :C].astype(F32)
-            up[...] = up_in[...].astype(F32)
-            out[...] = out_in[:, :C].astype(F32)
-            qkv[...] = qkv_in[...].astype(F32)
+        QW, AW = grad_rows - QKV, QKV - OUT
+        CUT = 192
+
+        def spread(small_in, io_in, grads_in, gain, rms, io, qkv, out, up, down, *refs):
+            held, io_held, wide, wide_up, wide_out, wide_down, isem, osem, csem = refs
+            io_load = pltpu.make_async_copy(io_in, io_held, csem.at[0])
+            io_copy = pltpu.make_async_copy(io_held, io, csem.at[1])
+
+            def load(i):
+                at = pl.ds(i * CUT, CUT)
+                return pltpu.make_async_copy(grads_in.at[at], held.at[at], isem.at[i])
+
+            for i in range(grad_rows // CUT):
+                load(i).start()
+            io_load.start()
             gain[...] = small_in[0:1, :]
             rms[0, 0] = jnp.max(small_in[1:2, :])
-
-        steps = 6
-        QW, AW = grad_rows - QKV, QKV - OUT
-        sizes = (FF // steps, D // steps, AW // steps, QW // steps)
-        firsts = (DOWN, UP, OUT, QKV)
-        piece_specs = [
-            pl.BlockSpec((n, D), lambda i, o=first // n: (o + i, 0))
-            for n, first in zip(sizes, firsts, strict=True)
-        ]
-        io_spec = pl.BlockSpec((1, R // 4, C), lambda i: (0, jnp.minimum(i, 3), 0))
-        whole = lambda i: (0, 0)
-        block_io, gain, grad_qkv, grad_out, grad_up, grad_down, rms = pl.pallas_call(
+            stores = []
+            for i in range(grad_rows // CUT):
+                load(i).wait()
+                at = i * CUT
+                for first, ref, dst in (
+                    (QKV, wide, qkv),
+                    (OUT, wide_out, out),
+                    (UP, wide_up, up),
+                    (DOWN, wide_down, down),
+                ):
+                    if at >= first:
+                        here = pl.ds(at - first, CUT)
+                        ref[here, :] = held[at : at + CUT, : ref.shape[1]].astype(F32)
+                        copy = pltpu.make_async_copy(ref.at[here], dst.at[here], osem.at[i])
+                        break
+                copy.start()
+                stores.append(copy)
+            io_load.wait()
+            io_copy.start()
+            for copy in stores:
+                copy.wait()
+            io_copy.wait()
+
+        shapes = ((QW, D), (AW, C), (D, FF), (FF, C))
+        cuts = grad_rows // CUT
+        gain, rms, block_io, grad_qkv, grad_out, grad_up, grad_down = pl.pallas_call(
             spread,
-            grid=(steps,),
             out_shape=(
+                jax.ShapeDtypeStruct((1, D), F32),
+                jax.ShapeDtypeStruct((1, 1), F32),
                 jax.ShapeDtypeStruct((1, R, C), BF),
-                jax.ShapeDtypeStruct((1, D), F32),
-                jax.ShapeDtypeStruct((QW, D), F32),
-                jax.ShapeDtypeStruct((AW, C), F32),
-                jax.ShapeDtypeStruct((D, FF), F32),
-                jax.ShapeDtypeStruct((FF, C), F32),
-                jax.ShapeDtypeStruct((1, 1), F32),
+                *(jax.ShapeDtypeStruct(shape, F32) for shape in shapes),
             ),
-            in_specs=[io_spec, *piece_specs, pl.BlockSpec((8, D), whole)],
-            out_specs=(
-                io_spec,
-                pl.BlockSpec((1, D), whole),
-                pl.BlockSpec((sizes[3], D), lambda i: (i, 0)),
-                pl.BlockSpec((sizes[2], C), lambda i: (i, 0)),
-                pl.BlockSpec((sizes[1], FF), lambda i: (i, 0)),
-                pl.BlockSpec((sizes[0], C), lambda i: (i, 0)),
-                smem,
-            ),
-        )(block_io, grads, grads, grads, grads, small)
+            in_specs=[vmem, anywhere, anywhere],
+            out_specs=(vmem, smem) + (anywhere,) * 5,
+            scratch_shapes=[
+                pltpu.VMEM((grad_rows, D), BF),
+                pltpu.VMEM((1, R, C), BF),
+                pltpu.VMEM((QW, D), F32),
+                pltpu.VMEM((D, FF), F32),
+                pltpu.VMEM((AW, C), F32),
+                pltpu.VMEM((FF, C), F32),
+                pltpu.SemaphoreType.DMA((cuts,)),
+                pltpu.SemaphoreType.DMA((cuts,)),
+                pltpu.SemaphoreType.DMA((2,)),
+            ],
+            compiler_params=pltpu.CompilerParams(vmem_limit_bytes=63 << 20),
+        )(small, block_io, grads)
         return (block_io, gain, grad_qkv.T, grad_out, grad_up, grad_down, rms.reshape(()))
 
     return run

time: 190 us -> 180 us (0.947); the launches traced: 187 us -> 180 us
  Pallas kernels: 187 us -> 179 us
    pallas_call x1, Pallas kernels: 179 us -> 173 us  [run(): pl.pallas_call(body, out_shape=(jax.ShapeDtypeStruct((1, R, C), BF), jax....]
where the time goes in v4:
time: 180 us
  Pallas kernels  179 us (99%)
    pallas_call x1, Pallas kernels, run(): pl.pallas_call(body, out_shape=(jax.ShapeDtypeStruct((1, R, C), BF), jax....  173 us
    pallas_call x1, Pallas kernels, run(): pl.pallas_call(spread, out_shape=(jax.ShapeDtypeStruct((1, D), F32), jax....  5.7 us

profile of v4, /device:TPU:0, one launch (start us, length us, event | category | flops | bytes accessed | tf_op | source)
XLA Modules:
  0.0 180.0 jit_solution(11824785853444139198)
XLA Ops:
  0.6 173.5 %shard_map.135 = (bf16[1,512,767]{2,1,0:T(8,128)(2,1)}, bf16[2304,768]{1,0:T(8,128)(2,1)}, f32[8,768]{1,0:T(8,128)}) custom-call(s32[4]{0:T(128)} %lens.1, f32[1,768]{1,0:T(1,128)} %gains.1, bf16[512,767]{1,0:T(8,128)(2,1)} %stream.1, bf16[512,767]{1,0:T(8,128)(2,1)} %cot_in.1, bf16[576,768]{1,0:T(8,128)(2,1)} %bitcast.3, bf16[192,767]{1,0:T(8,128)(2,1)} %w_ao.1, ...), custom_call_target="tpu_custom_call" | custom-call | tf_op jit(solution)/shard_map/pallas_call | solution.py:1091
  174.1 5.7 %shard_map.136 = (f32[1,768]{1,0:T(1,128)}, f32[1,1]{1,0:T(1,128)}, bf16[1,512,767]{2,1,0:T(8,128)(2,1)}, f32[576,768]{1,0:T(8,128)}, f32[192,767]{1,0:T(8,128)}...) custom-call(f32[8,768]{1,0:T(8,128)} %get-tuple-element.17.small_in, bf16[1,512,767]{2,1,0:T(8,128)(2,1)} %get-tuple-element.18.io_in, ...), custom_call_target="tpu_custom_call" | custom-call | tf_op jit(solution)/shard_map/pallas_call | solution.py:1148

commit v5 on v4

--- a/solution.py
+++ b/solution.py
@@ -13,10 +13,11 @@
 BF = jnp.bfloat16
 F32 = jnp.float32
 MESH = pl.DeviceIdType.MESH
-SUB = 48
+SUB = 32
+THIRD = 80
 LAG = 2
-BEFORE = (1, 2, 1, 1, 1)
-WITHIN = 6
+BEFORE = (1, 2, 1, 1, 0)
+WITHIN = 7
 ROOT = 0.7978845608028654
 
 
@@ -45,7 +46,7 @@
     QW = NH * 3 * HS
     AW = NH * HS
     GRADS = 2 * D + AW + QW
-    GROUPS = GRADS // (3 * SUB)
+    GROUPS = GRADS // (2 * SUB + THIRD)
     DOWN, UP, OUT, QKV = 0, FF, FF + D, FF + D + AW
     half_n = N // 2
 
@@ -55,7 +56,6 @@
         names[name] = pltpu.VMEM(shape, dtype)
 
     scratch("gbuf", (2, 8, D), F32)
-    scratch("stream", (R, C), BF)
     scratch("cot_in", (H, C), BF)
     scratch("wqkv", (QW, D), BF)
     scratch("wao_in", (AW, C), BF)
@@ -67,7 +67,7 @@
     scratch("n1", (4 * R, D), BF)
     scratch("q", (NH, 4 * R, HS), BF)
     scratch("k", (NH, 4 * R, HS), BF)
-    scratch("v", (NH, 4 * R, HS), BF)
+    scratch("v", (NH, 4 * R, 2 * HS), BF)
     scratch("e", (10 * NH, H, R), BF)
     scratch("il", (4 * H, 128), F32)
     scratch("att", (4 * H, AW), BF)
@@ -96,8 +96,8 @@
     scratch("rsxf", (R, D), BF)
     scratch("gsrc", (GRADS, D), BF)
     scratch("res", (GRADS, D), BF)
-    scratch("gb", ((GROUPS + -(-GROUPS // 4)) * SUB, D), BF)
-    scratch("gc", ((GROUPS + -(-GROUPS // 2)) * SUB, D), BF)
+    scratch("gb", (GROUPS * SUB + -(-GROUPS // 4) * THIRD, D), BF)
+    scratch("gc", (GROUPS * SUB + -(-GROUPS // 2) * THIRD, D), BF)
     scratch("sm", (5, 8, D), F32)
     scratch("smr", (3, 8, D), F32)
     scratch("smz", (N, 8, D), F32)
@@ -152,7 +152,7 @@
         loads = []
         for i, (src, dst) in enumerate(
             (
-                (stream, m.stream),
+                (stream, o_io.at[0]),
                 (w_qkv, m.wqkv),
                 (cot_in.at[rows(xh, H, H)], m.cot_in),
                 (w_ao, m.wao_in),
@@ -197,7 +197,7 @@
         loads[0].wait()
         own_rows = rows(t * R, R, R)
         m.n1[own_rows, D - 128 :] = jnp.zeros((R, 128), BF)
-        m.n1[own_rows, :C] = m.stream[...]
+        m.n1[own_rows, :C] = o_io[0]
         here = rows(t * H, H, H)
 
         half = H // 4
@@ -213,6 +213,9 @@
         part = m.cot.at[here]
         cot_core = send(part, part, core)
 
+        def turned(kb, h):
+            return rows((kb * NH + h) * HS, HS, HS)
+
         def qkv_rows(start):
             def step(i, _):
                 some = rows(start + i * 64, 64, 64)
@@ -228,7 +231,15 @@
                     part = mixed[:, (3 * h + p) * HS : (3 * h + p + 1) * HS]
                     if p == 0:
                         part = part * HS**-0.5
-                    ref[h, at, :] = part.astype(BF)
+                    part = part.astype(BF)
+                    if p == 2:
+                        ref[h, at, :HS] = part
+                        ref[h, at, HS:] = jnp.ones((H, HS), BF)
+                    else:
+                        ref[h, at, :] = part
+                    if p == 1:
+                        within = rows(lax.rem(start, R), H, H)
+                        m.act[turned(lax.div(start, R), h), within] = jnp.transpose(part)
 
         def qkv_block(block):
             lax.fori_loop(0, 2, lambda i, _: (qkv_rows(block * R + i * H), 0)[1], 0)
@@ -253,14 +264,21 @@
             fwd.append(send(part, part, core))
         part = m.cot.at[here]
         cot_y = send(part, part, ydev)
+        qkv_rows(t2 * R + xh)
+        for copy in fwd:
+            copy.wait_recv()
+        qkv_rows(t3 * R + xh)
+        passed = x_copies + fwd
+        fwd = []
         for k in range(4):
             x_copies[k].wait_recv()
             part = m.n1.at[rows(t2 * R + oh + k * half, half, half)]
             fwd.append(send(part, part, core))
-        qkv_block(t2)
+        qkv_rows(t2 * R + oh)
         for copy in fwd:
             copy.wait_recv()
-        qkv_block(t3)
+        qkv_rows(t3 * R + oh)
+        passed += fwd
 
         ends = [lens[0]]
         for i in range(1, 4):
@@ -283,7 +301,7 @@
             heads = [m.q[h, mine, :] for h in range(NH)]
 
             def scores(h, kb):
-                return dot_nt(heads[h], m.k[h, rows(kb * R, R, R), :])
+                return dot_nn(heads[h], m.act[turned(kb, h), :R])
 
             def top(s, best):
                 for g in lane_groups(s):
@@ -306,28 +324,25 @@
             best = [jnp.max(v, axis=1, keepdims=True) for v in best]
             between()
 
-            def weigh(h, kb, s, off, sums, acc):
-                e = jnp.exp(s - off)
-                for g in lane_groups(e):
-                    sums = sums + g
-                e = e.astype(BF)
+            def weigh(h, kb, s, off, acc):
+                e = jnp.exp(s - off).astype(BF)
                 m.e[unit(b, kb) * NH + h] = e
-                return sums, acc + dot_nn(e, m.v[h, rows(kb * R, R, R), :])
+                return acc + dot_nn(e, m.v[h, rows(kb * R, R, R), :])
 
             def add(kb, carry):
                 bias = bias_of(b, kb)
                 return tuple(
-                    weigh(h, kb, scores(h, kb), best[h] - bias, *carry[h]) for h in range(NH)
+                    weigh(h, kb, scores(h, kb), best[h] - bias, carry[h]) for h in range(NH)
                 )
 
-            zero = (jnp.zeros((H, 128), F32), jnp.zeros((H, HS), F32))
-            carry = tuple(weigh(h, b, masked(scores(h, b)), best[h], *zero) for h in range(NH))
+            zero = jnp.zeros((H, 2 * HS), F32)
+            carry = tuple(weigh(h, b, masked(scores(h, b)), best[h], zero) for h in range(NH))
             carry = lax.fori_loop(0, b, add, carry)
             at = rows(b * H, H, H)
             for h in range(NH):
-                inverse = 1.0 / total(carry[h][0])
+                inverse = 1.0 / carry[h][:, HS : HS + 1]
                 m.il[at, h : h + 1] = inverse
-                m.att[at, h * HS : (h + 1) * HS] = (carry[h][1] * inverse).astype(BF)
+                m.att[at, h * HS : (h + 1) * HS] = (carry[h][:, :HS] * inverse).astype(BF)
             return dot_nn(m.att[at, :], m.wao[...]).astype(BF)
 
         C_PROJ = counter[0]
@@ -390,11 +405,20 @@
         m.sm[0] = jnp.zeros((8, D), F32)
         m.sm[0, 2:3, :] = squares
 
-        n2_y = send(m.n2.at[here], m.n2.at[here], ydev)
+        C_N2Y = counter[0]
+        counter[0] += 6
+        side_rows = H // 2
+
+        def n2y_copy(k):
+            part = m.n2.at[rows(t * H + k * side_rows, side_rows, side_rows)]
+            return link(part, part, ydev, C_N2Y + k, C_N2Y + k)
+
+        n2y_copy(0).start()
+        n2y_copy(1).start()
         n2_core = send(m.n2.at[here], m.n2.at[here], core)
 
-        def feed(s, i):
-            at = rows(s * H, H, H)
+        def feed(start, count, i, to):
+            at = rows(start, count, count)
             for f in range(FF // 256):
                 cols = slice(f * 256, (f + 1) * 256)
                 hidden = dot_nn(m.n2[at, :], m.wup[:, cols])
@@ -407,54 +431,73 @@
                     1.0 + (3 * 0.044715) * square
                 )
                 m.gh[at, cols] = (grad * slope).astype(BF)
-            m.gp[i] = dot_nt(m.gh[at, :], m.wup[...]).astype(BF)
-
-        C_GP = counter[0]
+            m.gp[i, rows(to, count, count), :] = dot_nt(m.gh[at, :], m.wup[...]).astype(BF)
+
+        gp_near = link(m.gp.at[1], m.rsc2.at[0], core)
+        pending.append(gp_near)
+
+        def n2f_copy(k):
+            part = m.n2.at[rows(t2 * H + k * side_rows, side_rows, side_rows)]
+            return link(part, part, core, C_N2Y + 2 + k, C_N2Y + 2 + k)
+
+        def gp3_copy(k):
+            at = rows(k * side_rows, side_rows, side_rows)
+            return link(m.gp.at[3, at], m.rsc2.at[1, at], core, C_N2Y + 4 + k, C_N2Y + 4 + k)
+
+        C_GPY = counter[0]
         counter[0] += 2
-        C_N2 = counter[0]
-        counter[0] += 1
-        gp_copies = [
-            link(m.gp.at[2 * j + 1], m.rsc2.at[j], core, C_GP + j, C_GP + j) for j in range(2)
-        ]
-        part = m.n2.at[rows(t2 * H, H, H)]
-        n2_fwd = link(part, part, core, C_N2, C_N2)
-        pending.append(n2_fwd)
-        pending.extend(gp_copies)
-
-        def feed_step(i, _):
-            a, e = lax.div(i, 2), lax.rem(i, 2)
-            s = 2 * (y + a - 2 * y * a) + (c + e - 2 * c * e)
-
+
+        def gpy_copy(k):
+            at = rows(k * side_rows, side_rows, side_rows)
+            return link(m.ysnd2.at[at], m.rsy2.at[at], ydev, C_GPY + k, C_GPY + k)
+
+        def far_half(k):
+            gp3_copy(k).wait_recv()
+            at = rows(k * side_rows, side_rows, side_rows)
+            add_rows(m.ysnd2.at[at], (m.gp.at[2, at], m.rsc2.at[1, at]), side_rows)
+            gpy_copy(k).start()
+
+        def near_feed(i, _):
             @pl.when(i == 1)
             def _():
                 n2_core.wait_recv()
 
-            @pl.when(i == 2)
-            def _():
-                n2_y.wait_recv()
-                n2_fwd.start()
+            feed((2 * y + c + i - 2 * c * i) * H, H, i, 0)
+            return 0
+
+        def far_feed(q, _):
+            k, w = lax.div(q, 2), lax.rem(q, 2)
+
+            @pl.when(w == 0)
+            def _():
+                n2y_copy(k).wait_recv()
+                n2f_copy(k).start()
+
+            @pl.when(q == 0)
+            def _():
                 cot_fwd.wait_recv()
 
-            @pl.when(i == 3)
-            def _():
-                n2_fwd.wait_recv()
-
-            feed(s, i)
-
-            @pl.when(i == 1)
-            def _():
-                gp_copies[0].start()
-
-            @pl.when(i == 3)
-            def _():
-                gp_copies[1].start()
+            @pl.when(w == 1)
+            def _():
+                n2f_copy(k).wait_recv()
+
+            @pl.when(q == 3)
+            def _():
+                far_half(0)
+
+            s = 2 * (1 - y) + c + w - 2 * c * w
+            feed(s * H + k * side_rows, side_rows, 2 + w, k * side_rows)
+
+            @pl.when(w == 1)
+            def _():
+                gp3_copy(k).start()
 
             return 0
 
-        lax.fori_loop(0, 4, feed_step, 0)
-        gp_copies[1].wait_recv()
-        add_rows(m.ysnd2, (m.gp.at[2], m.rsc2.at[1]), H)
-        gp_y = send(m.ysnd2, m.rsy2, ydev)
+        lax.fori_loop(0, 2, near_feed, 0)
+        gp_near.start()
+        lax.fori_loop(0, 4, far_feed, 0)
+        far_half(1)
 
         is_mid = (d == half_n - 1) | (d == half_n)
         is_end = (d == 0) | (d == N - 1)
@@ -468,8 +511,17 @@
         def sub_rows(ref, at, count):
             return ref.at[rows(at, count * SUB, 16)]
 
+        def third_rows(ref, at):
+            return ref.at[rows(at, THIRD, 16)]
+
+        def b_third(g):
+            return third_rows(m.gb, GROUPS * SUB + lax.div(g, 4) * THIRD)
+
+        def c_third(g):
+            return third_rows(m.gc, GROUPS * SUB + lax.div(g, 2) * THIRD)
+
         def group_at(g):
-            return g * (3 * SUB)
+            return g * (2 * SUB + THIRD)
 
         def third_at(g):
             return group_at(g) + 2 * SUB
@@ -510,21 +562,21 @@
 
         def c_link(dst, dev, kind):
             def make(g):
-                src = sub_rows(m.gsrc, third_at(g), 1)
+                src = third_rows(m.gsrc, third_at(g))
                 return link(src, dst(g), dev, sem(6, g), sem(kind, g))
 
             return make
 
         def c_res(dev, kind):
             def make(g):
-                at = sub_rows(res, third_at(g), 1)
+                at = third_rows(res, third_at(g))
                 return link(at, at, dev, sem(kind, g), sem(8, g))
 
             return make
 
-        c_blk = c_link(lambda g: sub_rows(m.gc, (GROUPS + lax.div(g, 2)) * SUB, 1), xdev, 5)
-        c_in = c_link(lambda g: sub_rows(res, third_at(g), 1), inner, 6)
-        c_mid = c_link(lambda g: sub_rows(m.gb, (GROUPS + lax.div(g, 4)) * SUB, 1), inner, 7)
+        c_blk = c_link(c_third, xdev, 5)
+        c_in = c_link(lambda g: third_rows(res, third_at(g)), inner, 6)
+        c_mid = c_link(b_third, inner, 7)
         c_part, c_out, c_back = c_res(inner, 7), c_res(outer, 8), c_res(xdev, 9)
 
         def add(out, at, other, count):
@@ -533,6 +585,11 @@
                 there = other[k * SUB : (k + 1) * SUB, :].astype(F32)
                 out[here_rows, :] = (m.gsrc[here_rows, :].astype(F32) + there).astype(BF)
 
+        def add_third(out, g, other):
+            here_rows = rows(third_at(g), THIRD, 16)
+            both = m.gsrc[here_rows, :].astype(F32) + other[...].astype(F32)
+            out[here_rows, :] = both.astype(BF)
+
         def valid(g):
             return (g >= 0) & (g < GROUPS)
 
@@ -565,13 +622,13 @@
                 @pl.when(valid(g2) & mine(g2))
                 def _():
                     c_blk(g2).wait_recv()
-                    add(m.gsrc, third_at(g2), sub_rows(m.gc, (GROUPS + lax.div(g2, 2)) * SUB, 1), 1)
+                    add_third(m.gsrc, g2, c_third(g2))
                     if N > 4:
 
                         @pl.when(not_end)
                         def _():
                             c_in(g2).wait_recv()
-                            add(m.gsrc, third_at(g2), sub_rows(res, third_at(g2), 1), 1)
+                            add_third(m.gsrc, g2, third_rows(res, third_at(g2)))
 
                     c_in(g2).start()
 
@@ -612,7 +669,7 @@
                     @pl.when(mine(g2))
                     def _():
                         c_blk(g2).wait_recv()
-                        add(m.gsrc, third_at(g2), sub_rows(m.gc, (GROUPS + lax.div(g2, 2)) * SUB, 1), 1)
+                        add_third(m.gsrc, g2, c_third(g2))
 
                 @pl.when(valid(g3))
                 def _():
@@ -627,7 +684,7 @@
                             @pl.when(not_end)
                             def _():
                                 c_in(g3).wait_recv()
-                                add(m.gsrc, third_at(g3), sub_rows(res, third_at(g3), 1), 1)
+                                add_third(m.gsrc, g3, third_rows(res, third_at(g3)))
 
                         @pl.when(jnp.logical_not(late_owns(g3)))
                         def _():
@@ -647,7 +704,7 @@
                     @pl.when(mine(g4) & late_owns(g4))
                     def _():
                         c_mid(g4).wait_recv()
-                        add(res, third_at(g4), sub_rows(m.gb, (GROUPS + lax.div(g4, 4)) * SUB, 1), 1)
+                        add_third(res, g4, b_third(g4))
                         c_part(g4).start()
                         c_back(g4).start()
                         if N > 2:
@@ -679,7 +736,7 @@
             lax.fori_loop(begin, end, lambda s, _: (serve(s), 0)[1], 0)
 
         def leave(g):
-            at = rows(group_at(g), 3 * SUB, 16)
+            at = rows(group_at(g), 2 * SUB + THIRD, 16)
             return pltpu.make_async_copy(res.at[at], o_gr.at[at], osem.at[g])
 
         def settle(begin, end):
@@ -767,8 +824,9 @@
         mp_copies = [send(m.proj.at[2 * j + 1], m.rsc.at[j], core) for j in range(2)]
         serve_next(BEFORE[3])
 
-        gp_copies[0].wait_recv()
-        gp_y.wait_recv()
+        gp_near.wait_recv()
+        gpy_copy(0).wait_recv()
+        gpy_copy(1).wait_recv()
 
         def grad_middle_step(i, gain):
             at = rows(i * 64, 64, 64)
@@ -797,6 +855,18 @@
         pending.extend((gm_fwd, mp_y))
         gm_core.wait_recv()
 
+        def far_turned(kb, h):
+            return rows(2 * R * (1 - y) + (kb * NH + h) * HS, HS, HS)
+
+        def turn_values(i, _):
+            kb = lax.div(i, NH)
+            h = lax.rem(i, NH)
+            m.n1[far_turned(kb, h), :R] = jnp.transpose(m.v[h, rows(kb * R, R, R), :HS])
+            return 0
+
+        for copy in passed:
+            copy.wait_send()
+        lax.fori_loop(0, 4 * NH, turn_values, 0)
         def far_gradient():
             gm_y.wait_recv()
             gm_fwd.start()
@@ -872,7 +942,7 @@
                 for h in range(NH):
                     e = m.e[unit(b, kb) * NH + h]
                     at_k = rows(kb * R, R, R)
-                    dp = dot_nt(outs[h], m.v[h, at_k, :])
+                    dp = dot_nn(outs[h], m.n1[far_turned(kb, h), :R])
                     ds = (e.astype(F32) * (dp - offs[h])).astype(BF)
                     new.append(grads[h] + dot_nn(ds, m.k[h, at_k, :]))
                     m.dkt[kb, h] += dot_nn(q_ts[h], ds)
@@ -921,7 +991,8 @@
         tail[0] = BACK + WITHIN
         mp_copies[0].wait_recv()
         mp_y.wait_recv()
-        n2_y.wait_send()
+        n2y_copy(0).wait_send()
+        n2y_copy(1).wait_send()
         n2_core.wait_send()
         add_rows(m.n2.at[here], (m.mid, m.proj.at[0], m.rsc.at[0], m.rsy), H)
         bo_x = link(m.n2.at[here], m.gother, xdev)
@@ -1049,7 +1120,11 @@
 
         settle(settled, GROUPS)
         lax.fori_loop(0, GROUPS, lambda g, _: (leave(g).wait(), 0)[1], 0)
-        waited = {id(n2_y), id(n2_core), id(y_proj)}
+        waited = {id(copy) for copy in [n2_core, y_proj, *passed]}
+        for k in range(2):
+            n2f_copy(k).wait_send()
+            gp3_copy(k).wait_send()
+            gpy_copy(k).wait_send()
         for copy in pending:
             if id(copy) not in waited:
                 copy.wait_send()

time: 180 us -> 174 us (0.967)
  Pallas kernels: 179 us -> 173 us
    pallas_call x1, Pallas kernels: 173 us -> 167 us  [run(): pl.pallas_call(body, out_shape=(jax.ShapeDtypeStruct((1, R, C), BF), jax....]
where the time goes in v5:
time: 174 us
  Pallas kernels  173 us (99%)
    pallas_call x1, Pallas kernels, run(): pl.pallas_call(body, out_shape=(jax.ShapeDtypeStruct((1, R, C), BF), jax....  167 us
    pallas_call x1, Pallas kernels, run(): pl.pallas_call(spread, out_shape=(jax.ShapeDtypeStruct((1, D), F32), jax....  5.7 us

profile of v5, /device:TPU:0, one launch (start us, length us, event | category | flops | bytes accessed | tf_op | source)
XLA Modules:
  0.0 173.8 jit_solution(18259986462309918753)
XLA Ops:
  0.6 167.3 %shard_map.135 = (bf16[1,512,767]{2,1,0:T(8,128)(2,1)}, bf16[2304,768]{1,0:T(8,128)(2,1)}, f32[8,768]{1,0:T(8,128)}) custom-call(s32[4]{0:T(128)} %lens.1, f32[1,768]{1,0:T(1,128)} %gains.1, bf16[512,767]{1,0:T(8,128)(2,1)} %stream.1, bf16[512,767]{1,0:T(8,128)(2,1)} %cot_in.1, bf16[576,768]{1,0:T(8,128)(2,1)} %bitcast.3, bf16[192,767]{1,0:T(8,128)(2,1)} %w_ao.1, ...), custom_call_target="tpu_custom_call" | custom-call | tf_op jit(solution)/shard_map/pallas_call | solution.py:1166
  167.9 5.7 %shard_map.136 = (f32[1,768]{1,0:T(1,128)}, f32[1,1]{1,0:T(1,128)}, bf16[1,512,767]{2,1,0:T(8,128)(2,1)}, f32[576,768]{1,0:T(8,128)}, f32[192,767]{1,0:T(8,128)}...) custom-call(f32[8,768]{1,0:T(8,128)} %get-tuple-element.17.small_in, bf16[1,512,767]{2,1,0:T(8,128)(2,1)} %get-tuple-element.18.io_in, ...), custom_call_target="tpu_custom_call" | custom-call | tf_op jit(solution)/shard_map/pallas_call | solution.py:1223
